TPU v7x, 128 devices: a whole 4x4x4 slice. The times are simulated.
128 devices in a mesh: gx: 16 (over y, z), gy: 8 (over x, core).
Axes of the slice: x: 4, y: 4, z: 4, core: 2. Of those that a mesh axis runs over, the one named last changes fastest.
Arguments:
- atm_state: float32 [6, 4, 256, 4096], P(None, None, 'gy', 'gx'), may hold values from -6 to 6
- atm_kappa: float32 [6, 4], replicated, may hold values from 0.02 to 0.24
- intersection_weight: float32 [256, 4096], P('gy', 'gx'), may hold values from 0.1 to 0.5
- ocean_state: float32 [2, 8, 128, 2048], P(None, None, 'gy', 'gx'), may hold values from -6 to 6
- ocean_kappa: float32 [2, 8], replicated, may hold values from 0.02 to 0.12
- land_mask: int32 [128, 2048], P('gy', 'gx'), may hold values 0 or 1
- coupling_gain: float32 [2, 6], replicated, may hold values from -2.5 to 2.5
- send_map: int32 [8, 16, 16, 128], P('gy', 'gx'), may hold values from 0 to 2047, as said below
- recv_map: int32 [8, 16, 16, 128], P('gy', 'gx'), may hold values from 0 to 2047, as said below
- recv_count: int32 [8, 16, 16], P('gy', 'gx'), may hold values from 42 to 128, as said below
Outputs:
- atm_out: float32 [6, 4, 256, 4096], P(None, None, 'gy', 'gx')
- forcing: float32 [6, 128, 2048], P(None, 'gy', 'gx')
- ocean_out: float32 [2, 8, 128, 2048], P(None, None, 'gy', 'gx')
Inputs may be any that keep to these rules, and one draw needn't show every extreme that they name: For each row of tiles r, source s and destination d, send_map[r, s, d] lists every cell J * 128 + I of the source tile's ocean-resolution cells with d * 8 <= I < (d + 1) * 8 exactly once, in an order drawn from the seed. recv_map[r, d, s, k] names the same ocean cell as send_map[r, s, d, k], as the destination tile's local cell J * 128 + s * 8 + c. Only the first recv_count slots of a block take part; in every draw some row of tiles has a destination tile whose blocks from all sources are full.
All inputs are finite; a program needn't handle non-finite values. No bound on the sum of `land_mask` on one device may be relied on, other than what follows from the above.
Results may differ from a plain program's by a relative error of at most 0.00016.
Values sent between devices are 32-bit elements; how exact they have to be, the bound alone decides.
A program may use at most 64 MiB of HBM per device.

v0:
```python
import jax
import jax.numpy as jnp
from jax import lax
from jax.sharding import PartitionSpec as P

ASWEEPS = 6
OSWEEPS = 3


def with_halo(block, sides, width):
    for axis, dim in sides:
        count = lax.axis_size(axis)
        forward = [(i, i + 1) for i in range(count - 1)]
        forward.append((count - 1, 0))
        backward = [(target, source) for source, target in forward]
        low = lax.ppermute(
            lax.slice_in_dim(block, block.shape[dim] - width, None, axis=dim), axis, forward
        )
        high = lax.ppermute(lax.slice_in_dim(block, 0, width, axis=dim), axis, backward)
        block = jnp.concatenate([low, block, high], axis=dim)
    return block


def valid_rows(height, margin):
    rows = lax.axis_index("gy") * height - margin + jnp.arange(height + 2 * margin)
    inside = (rows >= 0) & (rows < height * lax.axis_size("gy"))
    return inside.astype(jnp.float32)


def atm_step(padded, diffusivity):
    center = padded[:, :, 1:-1, 1:-1]
    beside_all = (
        padded[:, :, 2:, 1:-1]
        + padded[:, :, :-2, 1:-1]
        + padded[:, :, 1:-1, 2:]
        + padded[:, :, 1:-1, :-2]
    )
    return center + diffusivity[:, :, None, None] * (beside_all - 4.0 * center)


def ocean_wide_step(padded, wet_padded, diffusivity):
    center = padded[..., 1:-1, :]
    wet_center = wet_padded[..., 1:-1, :]
    flux = wet_padded[..., 2:, :] * (padded[..., 2:, :] - center)
    flux = flux + wet_padded[..., :-2, :] * (padded[..., :-2, :] - center)
    flux = flux + jnp.roll(wet_center, -1, -1) * (jnp.roll(center, -1, -1) - center)
    flux = flux + jnp.roll(wet_center, 1, -1) * (jnp.roll(center, 1, -1) - center)
    return center + diffusivity[:, :, None, None] * wet_center * flux


def ocean_run(padded, wet_padded, diffusivity, margin):
    lead = padded.shape[:-2]
    field = padded.reshape(lead + (padded.shape[-2] * padded.shape[-1],))
    wet_field = wet_padded.reshape(
        wet_padded.shape[:-2] + (wet_padded.shape[-2] * wet_padded.shape[-1],)
    )
    field = ocean_wide_step(field, wet_field, diffusivity)
    field = field.reshape(field.shape[:-1] + padded.shape[-2:])
    return field[..., margin:-margin]


def fold_columns(padded, margin):
    first_tile = lax.axis_index("gx") == 0
    last_tile = lax.axis_index("gx") == lax.axis_size("gx") - 1
    left_band = padded[..., :margin]
    right_band = padded[..., -margin:]
    middle_band = padded[..., margin:-margin]
    left_band = jnp.where(first_tile, jnp.roll(left_band, 1, axis=-2), left_band)
    right_band = jnp.where(last_tile, jnp.roll(right_band, -1, axis=-2), right_band)
    return jnp.concatenate([left_band, middle_band, right_band], axis=-1)


def column_pairs(rows_part, select_even, select_odd):
    even_part = jnp.einsum("fyx,xc->fyc", rows_part, select_even, precision=lax.Precision.HIGHEST)
    odd_part = jnp.einsum("fyx,xc->fyc", rows_part, select_odd, precision=lax.Precision.HIGHEST)
    return (even_part, odd_part)


def per_device(
    atm_state,
    atm_kappa,
    intersection_weight,
    ocean_state,
    ocean_kappa,
    land_mask,
    coupling_gain,
    send_map,
    recv_map,
    recv_count,
):
    field_count, level_count, height, breadth = atm_state.shape
    tracer_count, depth_count, ocean_height, ocean_breadth = ocean_state.shape
    column_tiles = lax.axis_size("gx")
    block_width = ocean_breadth // column_tiles
    slot_count = send_map.shape[-1]
    field = atm_state
    for sweep_index in range(ASWEEPS):
        padded = with_halo(field, (("gx", 3), ("gy", 2)), 1)
        padded = padded * valid_rows(height, 1)[:, None]
        field = atm_step(padded, atm_kappa)
    surface = field[:, level_count - 1] * intersection_weight[None]
    paired_rows = surface.reshape(field_count, ocean_height, 2 * breadth)
    upper_rows = paired_rows[..., :breadth]
    lower_rows = paired_rows[..., breadth:]
    columns = jnp.arange(breadth, dtype=jnp.int32)[:, None]
    targets = 2 * jnp.arange(ocean_breadth, dtype=jnp.int32)[None, :]
    select_even = (columns == targets).astype(jnp.float32)
    select_odd = (columns == targets + 1).astype(jnp.float32)
    cell_index = send_map[0, 0]
    upper_even, upper_odd = column_pairs(upper_rows, select_even, select_odd)
    lower_even, lower_odd = column_pairs(lower_rows, select_even, select_odd)
    subcells = jnp.stack([upper_even, upper_odd, lower_even, lower_odd], axis=1)
    subcells = subcells.reshape(field_count, 4, ocean_height * ocean_breadth)
    outgoing = jnp.moveaxis(subcells[:, :, cell_index], 2, 0)
    received = lax.all_to_all(outgoing, "gx", split_axis=0, concat_axis=0, tiled=True)
    values = received.sum(axis=2)
    live_slots = (
        jnp.arange(slot_count, dtype=jnp.int32)[None, :] < recv_count[0, 0][:, None]
    ).astype(jnp.float32)
    values = values * live_slots[:, None, :]
    flat_values = jnp.moveaxis(values, 1, 0).reshape(field_count, -1)
    empty = jnp.zeros((field_count, ocean_height * ocean_breadth), jnp.float32)
    forcing_flat = empty.at[:, recv_map[0, 0].reshape(-1)].add(flat_values)
    forcing = forcing_flat.reshape(field_count, ocean_height, ocean_breadth)
    wet_stored = land_mask.astype(jnp.float32)
    blocked = ocean_state.reshape(
        tracer_count, depth_count, ocean_height, column_tiles, block_width
    )
    wet_blocked = wet_stored.reshape(1, 1, ocean_height, column_tiles, block_width)
    for sweep_index in range(OSWEEPS):
        padded, wet_padded = (
            with_halo(blocked, (("gx", 4), ("gy", 2)), 1),
            with_halo(wet_blocked, (("gx", 4), ("gy", 2)), 1),
        )
        padded = fold_columns(padded, 1)
        wet_padded = fold_columns(wet_padded, 1) * valid_rows(ocean_height, 1)[:, None, None]
        blocked = ocean_run(padded, wet_padded, ocean_kappa, 1)
    swept = blocked.reshape(tracer_count, depth_count, ocean_height, ocean_breadth)
    pushed = jnp.einsum("of,fyx->oyx", coupling_gain, forcing, precision=lax.Precision.HIGHEST)
    top_level = swept[:, 0] + wet_stored[None] * pushed
    ocean_out = swept.at[:, 0].set(top_level)
    return (field, forcing, ocean_out)


def solution(mesh):
    in_specs = (
        P(None, None, "gy", "gx"),
        P(),
        P("gy", "gx"),
        P(None, None, "gy", "gx"),
        P(),
        P("gy", "gx"),
        P(),
        P("gy", "gx", None, None),
        P("gy", "gx", None, None),
        P("gy", "gx", None),
    )
    out_specs = (P(None, None, "gy", "gx"), P(None, "gy", "gx"), P(None, None, "gy", "gx"))
    return jax.shard_map(
        per_device, mesh=mesh, in_specs=in_specs, out_specs=out_specs, check_vma=False
    )
```

profile of v0, /device:TPU:0, one launch (start us, length us, event | category | flops | bytes accessed | tf_op | source)
XLA Modules:
  0.0 336.2 jit_solution(6198805749437761116)
XLA Ops:
  3.6 4.7 %collective-permute-start.29 = (f32[1,1,16,16,1]{2,4,3,1,0:T(1,128)S(1)}, f32[1,1,16,16,1]{2,4,3,1,0:T(1,128)S(1)}, u32[]{:S(2)}, u32[]{:S(2)}) collective-permute-start(f32[1,1,16,16,1]{2,4,3,1,0:T(1,128)S(1)} %get-tuple-element.90), channel_id=1, source_target_pairs={{8,0},{16,8},{24,16},{32,24},{40,32},{48,40},{56,48},{64,56},{72,6... | collective-permute-start | bytes 3080 | tf_op jit(solution)/shard_map/ppermute | solution.py:19
  10.4 5.3 %collective-permute-start.1 = (f32[6,4,32,1]{3,2,1,0:T(8,128)}, f32[6,4,32,1]{3,2,1,0:T(8,128)}, u32[]{:S(2)}, u32[]{:S(2)}) collective-permute-start(f32[6,4,32,1]{3,2,1,0:T(8,128)} %get-tuple-element.86), channel_id=1, source_target_pairs={{8,0},{16,8},{24,16},{32,24},{40,32},{48,40},{56,48},{64,56},{72,6... | collective-permute-start | bytes 9224 | tf_op jit(solution)/shard_map/ppermute | solution.py:19
  26.4 5.8 %collective-permute-start.25 = (f32[2,8,16,16,1]{2,4,3,1,0:T(1,128)S(1)}, f32[2,8,16,16,1]{2,4,3,1,0:T(1,128)S(1)}, u32[]{:S(2)}, u32[]{:S(2)}) collective-permute-start(f32[2,8,16,16,1]{2,4,3,1,0:T(1,128)S(1)} %get-tuple-element.74), channel_id=1, source_target_pairs={{8,0},{16,8},{24,16},{32,24},{40,32},{48,40},{56,48},{64,56},{72,6... | collective-permute-start | bytes 49160 | tf_op jit(solution)/shard_map/ppermute | solution.py:19
  38.3 3.2 copy.199
  50.2 3.3 copy.202
  53.5 3.3 pad_maximum_fusion.2
  77.4 3.2 fusion.72
  90.4 4.8 %collective-permute-start.33 = (f32[2,8,16,16,1]{2,4,3,1,0:T(1,128)}, f32[2,8,16,16,1]{2,4,3,1,0:T(1,128)S(1)}, u32[]{:S(2)}, u32[]{:S(2)}) collective-permute-start(f32[2,8,16,16,1]{2,4,3,1,0:T(1,128)} %copy.272), channel_id=1, source_target_pairs={{8,0},{16,8},{24,16},{32,24},{40,32},{48,40},{56,48},{64,56},{72,6... | collective-permute-start | bytes 49160 | tf_op jit(solution)/shard_map/ppermute | solution.py:19
  99.2 5.5 %collective-permute-start.5 = (f32[6,4,32,1]{3,2,1,0:T(8,128)S(1)}, f32[6,4,32,1]{3,2,1,0:T(8,128)S(1)}, u32[]{:S(2)}, u32[]{:S(2)}) collective-permute-start(f32[6,4,32,1]{3,2,1,0:T(8,128)S(1)} %get-tuple-element.84), channel_id=1, source_target_pairs={{8,0},{16,8},{24,16},{32,24},{40,32},{48,40},{56,48},{64,56},{72,6... | collective-permute-start | bytes 9224 | tf_op jit(solution)/shard_map/ppermute | solution.py:19
  120.3 3.3 copy.219
  123.5 3.3 pad_maximum_fusion.5
  155.2 3.3 copy.280
  167.1 5.5 %collective-permute-start.9 = (f32[6,4,32,1]{3,2,1,0:T(8,128)S(1)}, f32[6,4,32,1]{3,2,1,0:T(8,128)S(1)}, u32[]{:S(2)}, u32[]{:S(2)}) collective-permute-start(f32[6,4,32,1]{3,2,1,0:T(8,128)S(1)} %get-tuple-element.82), channel_id=1, source_target_pairs={{8,0},{16,8},{24,16},{32,24},{40,32},{48,40},{56,48},{64,56},{72,6... | collective-permute-start | bytes 9224 | tf_op jit(solution)/shard_map/ppermute | solution.py:19
  188.5 3.3 copy.234
  197.4 5.5 %collective-permute-start.13 = (f32[6,4,32,1]{3,2,1,0:T(8,128)S(1)}, f32[6,4,32,1]{3,2,1,0:T(8,128)S(1)}, u32[]{:S(2)}, u32[]{:S(2)}) collective-permute-start(f32[6,4,32,1]{3,2,1,0:T(8,128)S(1)} %get-tuple-element.80), channel_id=1, source_target_pairs={{8,0},{16,8},{24,16},{32,24},{40,32},{48,40},{56,48},{64,56},{72,6... | collective-permute-start | bytes 9224 | tf_op jit(solution)/shard_map/ppermute | solution.py:19
  204.1 4.4 %collective-permute-done.12 = f32[6,4,32,1]{3,2,1,0:T(8,128)S(1)} collective-permute-done((f32[6,4,32,1]{3,2,1,0:T(8,128)S(1)}, f32[6,4,32,1]{3,2,1,0:T(8,128)S(1)}, u32[]{:S(2)}, u32[]{:S(2)}) %collective-permute-start.12) | collective-permute-done | bytes 3104 | tf_op jit(solution)/shard_map/ppermute | solution.py:16
  215.4 5.5 %collective-permute-start.17 = (f32[6,4,32,1]{3,2,1,0:T(8,128)S(1)}, f32[6,4,32,1]{3,2,1,0:T(8,128)S(1)}, u32[]{:S(2)}, u32[]{:S(2)}) collective-permute-start(f32[6,4,32,1]{3,2,1,0:T(8,128)S(1)} %get-tuple-element.78), channel_id=1, source_target_pairs={{8,0},{16,8},{24,16},{32,24},{40,32},{48,40},{56,48},{64,56},{72,6... | collective-permute-start | bytes 9224 | tf_op jit(solution)/shard_map/ppermute | solution.py:19
  222.2 6.6 %collective-permute-done.16 = f32[6,4,32,1]{3,2,1,0:T(8,128)S(1)} collective-permute-done((f32[6,4,32,1]{3,2,1,0:T(8,128)S(1)}, f32[6,4,32,1]{3,2,1,0:T(8,128)S(1)}, u32[]{:S(2)}, u32[]{:S(2)}) %collective-permute-start.16) | collective-permute-done | bytes 3104 | tf_op jit(solution)/shard_map/ppermute | solution.py:16
  235.8 5.7 %collective-permute-start.21 = (f32[6,4,32,1]{3,2,1,0:T(8,128)S(1)}, f32[6,4,32,1]{3,2,1,0:T(8,128)S(1)}, u32[]{:S(2)}, u32[]{:S(2)}) collective-permute-start(f32[6,4,32,1]{3,2,1,0:T(8,128)S(1)} %get-tuple-element.76), channel_id=1, source_target_pairs={{8,0},{16,8},{24,16},{32,24},{40,32},{48,40},{56,48},{64,56},{72,6... | collective-permute-start | bytes 9224 | tf_op jit(solution)/shard_map/ppermute | solution.py:19
  243.7 6.0 %collective-permute-done.20 = f32[6,4,32,1]{3,2,1,0:T(8,128)S(1)} collective-permute-done((f32[6,4,32,1]{3,2,1,0:T(8,128)S(1)}, f32[6,4,32,1]{3,2,1,0:T(8,128)S(1)}, u32[]{:S(2)}, u32[]{:S(2)}) %collective-permute-start.20) | collective-permute-done | bytes 3104 | tf_op jit(solution)/shard_map/ppermute | solution.py:16
  276.3 7.3 %pad_maximum_fusion = f32[6,4,2048]{0,1,2:T(4,128)} fusion(f32[6,1,2048]{0,1,2:T(1,128)S(1)} %bitcast.93, f32[6,1,2048]{0,1,2:T(1,128)S(1)} %bitcast.92, f32[6,1,2048]{0,1,2:T(1,128)} %bitcast.94, f32[6,1,2048]{0,1,2:T(1,128)S(1)} %bitcast.91), kind=kLoop, calls=%fused_computation.2 | loop fusion | flops 147456 | bytes 393216 | tf_op jit(solution)/shard_map/stack | solution.py:112
  283.6 17.8 %gather_fusion = f32[2048,6,4]{1,2,0:T(4,128)} fusion(f32[6,4,2048]{0,1,2:T(4,128)} %pad_maximum_fusion, s32[2048]{0:T(1024)} %fusion.64), kind=kCustom, calls=%fused_computation | custom fusion | bytes 401408 | tf_op jit(solution)/shard_map/gather | solution.py:114
  305.2 7.0 %all-to-all-start = ((f32[16,6,4,128]{3,2,1,0:T(4,128)}), f32[16,6,4,128]{3,2,1,0:T(4,128)S(1)}, u32[]{:S(2)}, u32[]{:S(2)}) async-start(f32[16,6,4,128]{3,2,1,0:T(4,128)} %copy.195), calls=%async_computation | async-start | bytes 393216 | tf_op jit(solution)/shard_map/all_to_all | solution.py:115
  320.8 11.8 %scatter_custom_fusion = f32[6,2048]{0,1:T(8,128)S(1)} fusion(s32[2048]{0:T(1024)} %bitcast.112, f32[2048,6]{1,0:T(8,128)S(1)} %bitcast.100, f32[]{:T(128)} %constant.58.clone.1), kind=kCustom, calls=%fused_computation.58 | custom fusion | flops 12288 | bytes 49664 | tf_op jit(solution)/shard_map/scatter-add | solution.py:123
  (308 shorter events, 198.5 us)
Async XLA Ops:
  1.5 19.1 %collective-permute-start.28 = (f32[1,1,16,16,1]{2,4,3,1,0:T(1,128)S(1)}, f32[1,1,16,16,1]{2,4,3,1,0:T(1,128)S(1)}, u32[]{:S(2)}, u32[]{:S(2)}) collective-permute-start(f32[1,1,16,16,1]{2,4,3,1,0:T(1,128)S(1)} %get-tuple-element.89), channel_id=1, source_target_pairs={{0,8},{8,16},{16,24},{24,32},{32,40},{40,48},{48,56},{56,64},{64,7... | collective-permute-start | bytes 3080 | tf_op jit(solution)/shard_map/ppermute | solution.py:16
  3.6 17.1 %collective-permute-start.29 = (f32[1,1,16,16,1]{2,4,3,1,0:T(1,128)S(1)}, f32[1,1,16,16,1]{2,4,3,1,0:T(1,128)S(1)}, u32[]{:S(2)}, u32[]{:S(2)}) collective-permute-start(f32[1,1,16,16,1]{2,4,3,1,0:T(1,128)S(1)} %get-tuple-element.90), channel_id=1, source_target_pairs={{8,0},{16,8},{24,16},{32,24},{40,32},{48,40},{56,48},{64,56},{72,6... | collective-permute-start | bytes 3080 | tf_op jit(solution)/shard_map/ppermute | solution.py:19
  10.4 32.8 %collective-permute-start = (f32[6,4,32,1]{3,2,1,0:T(8,128)}, f32[6,4,32,1]{3,2,1,0:T(8,128)}, u32[]{:S(2)}, u32[]{:S(2)}) collective-permute-start(f32[6,4,32,1]{3,2,1,0:T(8,128)} %get-tuple-element.85), channel_id=1, source_target_pairs={{0,8},{8,16},{16,24},{24,32},{32,40},{40,48},{48,56},{56,64},{64,7... | collective-permute-start | bytes 9224 | tf_op jit(solution)/shard_map/ppermute | solution.py:16
  10.4 32.8 %collective-permute-start.1 = (f32[6,4,32,1]{3,2,1,0:T(8,128)}, f32[6,4,32,1]{3,2,1,0:T(8,128)}, u32[]{:S(2)}, u32[]{:S(2)}) collective-permute-start(f32[6,4,32,1]{3,2,1,0:T(8,128)} %get-tuple-element.86), channel_id=1, source_target_pairs={{8,0},{16,8},{24,16},{32,24},{40,32},{48,40},{56,48},{64,56},{72,6... | collective-permute-start | bytes 9224 | tf_op jit(solution)/shard_map/ppermute | solution.py:19
  17.1 18.6 %collective-permute-start.24 = (f32[2,8,16,16,1]{2,4,3,1,0:T(1,128)S(1)}, f32[2,8,16,16,1]{2,4,3,1,0:T(1,128)S(1)}, u32[]{:S(2)}, u32[]{:S(2)}) collective-permute-start(f32[2,8,16,16,1]{2,4,3,1,0:T(1,128)S(1)} %get-tuple-element.73), channel_id=1, source_target_pairs={{0,8},{8,16},{16,24},{24,32},{32,40},{40,48},{48,56},{56,64},{64,7... | collective-permute-start | bytes 49160 | tf_op jit(solution)/shard_map/ppermute | solution.py:16
  20.8 11.4 %collective-permute-start.31 = (f32[1,1,1,16,10]{2,4,3,1,0:T(8,128)S(1)}, f32[1,1,1,16,10]{2,4,3,1,0:T(8,128)S(1)}, u32[]{:S(2)}, u32[]{:S(2)}) collective-permute-start(f32[1,1,1,16,10]{2,4,3,1,0:T(8,128)S(1)} %get-tuple-element.88), channel_id=1, source_target_pairs={{1,0},{2,1},{3,2},{4,3},{5,4},{6,5},{7,6},{0,7},{9,8},{10,9},{11,1... | collective-permute-start | bytes 1928 | tf_op jit(solution)/shard_map/ppermute | solution.py:19
  45.3 50.0 %collective-permute-start.2 = (f32[6,4,1,258]{3,2,1,0:T(1,128)}, f32[6,4,1,258]{3,2,1,0:T(1,128)}, u32[]{:S(2)}, u32[]{:S(2)}) collective-permute-start(f32[6,4,1,258]{3,2,1,0:T(1,128)} %get-tuple-element.50), channel_id=1, source_target_pairs={{0,1},{1,2},{2,3},{3,4},{4,5},{5,6},{6,7},{7,0},{8,9},{9,10},{10,1... | collective-permute-start | bytes 74312 | tf_op jit(solution)/shard_map/ppermute | solution.py:16
  45.3 50.0 %collective-permute-start.3 = (f32[6,4,1,258]{3,2,1,0:T(1,128)}, f32[6,4,1,258]{3,2,1,0:T(1,128)}, u32[]{:S(2)}, u32[]{:S(2)}) collective-permute-start(f32[6,4,1,258]{3,2,1,0:T(1,128)} %get-tuple-element.51), channel_id=1, source_target_pairs={{1,0},{2,1},{3,2},{4,3},{5,4},{6,5},{7,6},{0,7},{9,8},{10,9},{11,1... | collective-permute-start | bytes 74312 | tf_op jit(solution)/shard_map/ppermute | solution.py:19
  90.4 14.3 %collective-permute-start.33 = (f32[2,8,16,16,1]{2,4,3,1,0:T(1,128)}, f32[2,8,16,16,1]{2,4,3,1,0:T(1,128)S(1)}, u32[]{:S(2)}, u32[]{:S(2)}) collective-permute-start(f32[2,8,16,16,1]{2,4,3,1,0:T(1,128)} %copy.272), channel_id=1, source_target_pairs={{8,0},{16,8},{24,16},{32,24},{40,32},{48,40},{56,48},{64,56},{72,6... | collective-permute-start | bytes 49160 | tf_op jit(solution)/shard_map/ppermute | solution.py:19
  99.2 14.5 %collective-permute-start.4 = (f32[6,4,32,1]{3,2,1,0:T(8,128)}, f32[6,4,32,1]{3,2,1,0:T(8,128)S(1)}, u32[]{:S(2)}, u32[]{:S(2)}) collective-permute-start(f32[6,4,32,1]{3,2,1,0:T(8,128)} %get-tuple-element.83), channel_id=1, source_target_pairs={{0,8},{8,16},{16,24},{24,32},{32,40},{40,48},{48,56},{56,64},{64,7... | collective-permute-start | bytes 9224 | tf_op jit(solution)/shard_map/ppermute | solution.py:16
  99.2 14.5 %collective-permute-start.5 = (f32[6,4,32,1]{3,2,1,0:T(8,128)S(1)}, f32[6,4,32,1]{3,2,1,0:T(8,128)S(1)}, u32[]{:S(2)}, u32[]{:S(2)}) collective-permute-start(f32[6,4,32,1]{3,2,1,0:T(8,128)S(1)} %get-tuple-element.84), channel_id=1, source_target_pairs={{8,0},{16,8},{24,16},{32,24},{40,32},{48,40},{56,48},{64,56},{72,6... | collective-permute-start | bytes 9224 | tf_op jit(solution)/shard_map/ppermute | solution.py:19
  114.6 49.1 %collective-permute-start.6 = (f32[6,4,1,258]{3,2,1,0:T(1,128)}, f32[6,4,1,258]{3,2,1,0:T(1,128)}, u32[]{:S(2)}, u32[]{:S(2)}) collective-permute-start(f32[6,4,1,258]{3,2,1,0:T(1,128)} %get-tuple-element.48), channel_id=1, source_target_pairs={{0,1},{1,2},{2,3},{3,4},{4,5},{5,6},{6,7},{7,0},{8,9},{9,10},{10,1... | collective-permute-start | bytes 74312 | tf_op jit(solution)/shard_map/ppermute | solution.py:16
  114.6 49.1 %collective-permute-start.7 = (f32[6,4,1,258]{3,2,1,0:T(1,128)}, f32[6,4,1,258]{3,2,1,0:T(1,128)}, u32[]{:S(2)}, u32[]{:S(2)}) collective-permute-start(f32[6,4,1,258]{3,2,1,0:T(1,128)} %get-tuple-element.49), channel_id=1, source_target_pairs={{1,0},{2,1},{3,2},{4,3},{5,4},{6,5},{7,6},{0,7},{9,8},{10,9},{11,1... | collective-permute-start | bytes 74312 | tf_op jit(solution)/shard_map/ppermute | solution.py:19
  167.1 14.8 %collective-permute-start.8 = (f32[6,4,32,1]{3,2,1,0:T(8,128)}, f32[6,4,32,1]{3,2,1,0:T(8,128)S(1)}, u32[]{:S(2)}, u32[]{:S(2)}) collective-permute-start(f32[6,4,32,1]{3,2,1,0:T(8,128)} %get-tuple-element.81), channel_id=1, source_target_pairs={{0,8},{8,16},{16,24},{24,32},{32,40},{40,48},{48,56},{56,64},{64,7... | collective-permute-start | bytes 9224 | tf_op jit(solution)/shard_map/ppermute | solution.py:16
  167.1 14.8 %collective-permute-start.9 = (f32[6,4,32,1]{3,2,1,0:T(8,128)S(1)}, f32[6,4,32,1]{3,2,1,0:T(8,128)S(1)}, u32[]{:S(2)}, u32[]{:S(2)}) collective-permute-start(f32[6,4,32,1]{3,2,1,0:T(8,128)S(1)} %get-tuple-element.82), channel_id=1, source_target_pairs={{8,0},{16,8},{24,16},{32,24},{40,32},{48,40},{56,48},{64,56},{72,6... | collective-permute-start | bytes 9224 | tf_op jit(solution)/shard_map/ppermute | solution.py:19
  182.8 11.9 %collective-permute-start.10 = (f32[6,4,1,258]{3,2,1,0:T(1,128)}, f32[6,4,1,258]{3,2,1,0:T(1,128)}, u32[]{:S(2)}, u32[]{:S(2)}) collective-permute-start(f32[6,4,1,258]{3,2,1,0:T(1,128)} %get-tuple-element.46), channel_id=1, source_target_pairs={{0,1},{1,2},{2,3},{3,4},{4,5},{5,6},{6,7},{7,0},{8,9},{9,10},{10,1... | collective-permute-start | bytes 74312 | tf_op jit(solution)/shard_map/ppermute | solution.py:16
  182.8 11.9 %collective-permute-start.11 = (f32[6,4,1,258]{3,2,1,0:T(1,128)S(1)}, f32[6,4,1,258]{3,2,1,0:T(1,128)}, u32[]{:S(2)}, u32[]{:S(2)}) collective-permute-start(f32[6,4,1,258]{3,2,1,0:T(1,128)S(1)} %get-tuple-element.47), channel_id=1, source_target_pairs={{1,0},{2,1},{3,2},{4,3},{5,4},{6,5},{7,6},{0,7},{9,8},{10,9},{11,1... | collective-permute-start | bytes 74312 | tf_op jit(solution)/shard_map/ppermute | solution.py:19
  215.3 13.5 %collective-permute-start.16 = (f32[6,4,32,1]{3,2,1,0:T(8,128)S(1)}, f32[6,4,32,1]{3,2,1,0:T(8,128)S(1)}, u32[]{:S(2)}, u32[]{:S(2)}) collective-permute-start(f32[6,4,32,1]{3,2,1,0:T(8,128)S(1)} %get-tuple-element.77), channel_id=1, source_target_pairs={{0,8},{8,16},{16,24},{24,32},{32,40},{40,48},{48,56},{56,64},{64,7... | collective-permute-start | bytes 9224 | tf_op jit(solution)/shard_map/ppermute | solution.py:16
  215.4 13.4 %collective-permute-start.17 = (f32[6,4,32,1]{3,2,1,0:T(8,128)S(1)}, f32[6,4,32,1]{3,2,1,0:T(8,128)S(1)}, u32[]{:S(2)}, u32[]{:S(2)}) collective-permute-start(f32[6,4,32,1]{3,2,1,0:T(8,128)S(1)} %get-tuple-element.78), channel_id=1, source_target_pairs={{8,0},{16,8},{24,16},{32,24},{40,32},{48,40},{56,48},{64,56},{72,6... | collective-permute-start | bytes 9224 | tf_op jit(solution)/shard_map/ppermute | solution.py:19
  235.7 14.0 %collective-permute-start.20 = (f32[6,4,32,1]{3,2,1,0:T(8,128)S(1)}, f32[6,4,32,1]{3,2,1,0:T(8,128)S(1)}, u32[]{:S(2)}, u32[]{:S(2)}) collective-permute-start(f32[6,4,32,1]{3,2,1,0:T(8,128)S(1)} %get-tuple-element.75), channel_id=1, source_target_pairs={{0,8},{8,16},{16,24},{24,32},{32,40},{40,48},{48,56},{56,64},{64,7... | collective-permute-start | bytes 9224 | tf_op jit(solution)/shard_map/ppermute | solution.py:16
  235.8 14.0 %collective-permute-start.21 = (f32[6,4,32,1]{3,2,1,0:T(8,128)S(1)}, f32[6,4,32,1]{3,2,1,0:T(8,128)S(1)}, u32[]{:S(2)}, u32[]{:S(2)}) collective-permute-start(f32[6,4,32,1]{3,2,1,0:T(8,128)S(1)} %get-tuple-element.76), channel_id=1, source_target_pairs={{8,0},{16,8},{24,16},{32,24},{40,32},{48,40},{56,48},{64,56},{72,6... | collective-permute-start | bytes 9224 | tf_op jit(solution)/shard_map/ppermute | solution.py:19
  250.6 15.8 %collective-permute-start.22 = (f32[6,4,1,258]{3,2,1,0:T(1,128)}, f32[6,4,1,258]{3,2,1,0:T(1,128)}, u32[]{:S(2)}, u32[]{:S(2)}) collective-permute-start(f32[6,4,1,258]{3,2,1,0:T(1,128)} %get-tuple-element.40), channel_id=1, source_target_pairs={{0,1},{1,2},{2,3},{3,4},{4,5},{5,6},{6,7},{7,0},{8,9},{9,10},{10,1... | collective-permute-start | bytes 74312 | tf_op jit(solution)/shard_map/ppermute | solution.py:16
  250.6 15.8 %collective-permute-start.23 = (f32[6,4,1,258]{3,2,1,0:T(1,128)}, f32[6,4,1,258]{3,2,1,0:T(1,128)}, u32[]{:S(2)}, u32[]{:S(2)}) collective-permute-start(f32[6,4,1,258]{3,2,1,0:T(1,128)} %get-tuple-element.41), channel_id=1, source_target_pairs={{1,0},{2,1},{3,2},{4,3},{5,4},{6,5},{7,6},{0,7},{9,8},{10,9},{11,1... | collective-permute-start | bytes 74312 | tf_op jit(solution)/shard_map/ppermute | solution.py:19
  305.2 15.1 %all-to-all-start = ((f32[16,6,4,128]{3,2,1,0:T(4,128)}), f32[16,6,4,128]{3,2,1,0:T(4,128)S(1)}, u32[]{:S(2)}, u32[]{:S(2)}) async-start(f32[16,6,4,128]{3,2,1,0:T(4,128)} %copy.195), calls=%async_computation | async-start | bytes 393216 | tf_op jit(solution)/shard_map/all_to_all | solution.py:115
  (59 other events, 808.0 us)
where the time goes:
time: 340 us; the launch traced here: 336 us
  local copies, waits for them, and re-layouts  160 us (47%)
  starting transfers between devices  82.1 us (24%)
  other arithmetic  65.9 us (19%)
  waiting for transfers between devices  23.1 us (7%)
    ppermute x20, starting transfers between devices, with_halo(): lax.ppermute(lax.slice_in_dim(block, 0, width, axis=dim), axis, backward)  71.1 us
    unnamed x120, local copies, waits for them, and re-layouts  56.2 us
    slice x17, local copies, waits for them, and re-layouts, with_halo(): lax.slice_in_dim(block, block.shape[dim] - width, None, axis=dim)  27.2 us
    ppermute x20, waiting for transfers between devices, with_halo(): lax.ppermute(lax.slice_in_dim(block, block.shape[dim] - width, None, axis...  20.9 us
    gather x2, local copies, waits for them, and re-layouts, per_device(): outgoing = jnp.moveaxis(subcells[:, :, cell_index], 2, 0)  20.7 us
    scatter-add x1, other arithmetic, per_device(): forcing_flat = empty.at[:, recv_map[0, 0].reshape(-1)].add(flat_values)  11.8 us
    concatenate x8, other arithmetic, with_halo(): block = jnp.concatenate([low, block, high], axis=dim)  10 us
    ppermute x3, local copies, waits for them, and re-layouts, with_halo(): lax.ppermute(lax.slice_in_dim(block, 0, width, axis=dim), axis, backward)  9.76 us
  transfers between devices with their start and end apart: 41, of which 8 were waited for; matrix products, arithmetic and copies ran while one was open for 49% of the time, Pallas kernels for 0%

commit v1 on v0

v1 whole, which is shorter than its diff:
```python
import jax
import jax.numpy as jnp
from jax import lax
from jax.experimental import pallas as pl
from jax.experimental.pallas import tpu as pltpu
from jax.sharding import PartitionSpec as P

ASWEEPS = 6
OSWEEPS = 3
VARS, LEV = 6, 4
OVARS, OLEV = 2, 8
GX, GY = 16, 8
ROWS, COLS = 32, 256
OROWS, OCOLS = 16, 128
EXT = ROWS + 2 * ASWEEPS
OEXT = OROWS + 2 * OSWEEPS
MESH = pl.DeviceIdType.MESH

ORDER = (
    [(v, 3) for v in range(6)]
    + [(v, 0) for v in range(6)]
    + [(v, 1) for v in range(6)]
    + [(v, 2) for v in range(6)]
)
RUNS = ((0, 0, 6, 3), (6, 0, 2, 0), (8, 2, 4, 0), (12, 0, 6, 1), (18, 0, 6, 2))

G0_TOP, G0_BOT, G0_RIGHT, G0_LEFT, G0_DIAG = 0, 1, 2, 3, 4
GR_TOP, GR_BOT, SIDE_RIGHT, SIDE_LEFT, SIDE_DIAG = 8, 9, 10, 11, 12
OC_TOP, OC_BOT = 16, 17
N_HALO = 18
HALF_AT = (5, 7, 29, 31)


def body(
    kappa, okappa, gain, rcnt,
    atm, iw_in, oce, mask_in, rmap_in,
    atm_out, forc_out, oce_out,
    stage, ostage, iw, maskv, rmap,
    a0, a1, a2,
    gsl, gsr, grr, grl,
    sl, sr, rr, rl,
    su, sd, ru, rd,
    c0, h0, c1, h1, c2, h2,
    mnat, ko, live,
    xs, msg, got,
    outst, oout, fout,
    in_sem, out_sem, hs_sem, hr_sem, as_sem, ar_sem,
):
    gx = lax.axis_index("gx")
    gy = lax.axis_index("gy")
    right, left = lax.rem(gx + 1, GX), lax.rem(gx + GX - 1, GX)
    down, up = lax.rem(gy + 1, GY), lax.rem(gy + GY - 1, GY)

    def run_in(n):
        p, v, cnt, l = RUNS[n]
        return [
            pltpu.make_async_copy(
                atm.at[pl.ds(v, cnt), l, :, pl.ds(128 * t, 128)],
                stage.at[t, pl.ds(p, cnt)],
                in_sem.at[2 * n + t],
            )
            for t in range(2)
        ]

    ins = [run_in(n) for n in range(5)]
    for n in (0, 1):
        for c in ins[n]:
            c.start()
    ocopy = pltpu.make_async_copy(oce, ostage, in_sem.at[10])
    wcopy = pltpu.make_async_copy(iw_in, iw, in_sem.at[11])
    mcopy = pltpu.make_async_copy(mask_in, maskv, in_sem.at[12])
    rcopy = pltpu.make_async_copy(rmap_in, rmap, in_sem.at[13])

    barrier = pltpu.get_barrier_semaphore()

    def greet(a, b):
        pl.semaphore_signal(
            barrier, inc=1, device_id={"gx": a, "gy": b}, device_id_type=MESH
        )

    for a in (left, gx, right):
        for b in (up, gy, down):
            if a is gx and b is gy:
                continue
            greet(a, b)
    for k in range(2, GX - 1):
        greet(lax.rem(gx + k, GX), gy)

    for n in (2, 3, 4):
        for c in ins[n]:
            c.start()
    for c in (ocopy, mcopy, wcopy, rcopy):
        c.start()

    lane = lax.broadcasted_iota(jnp.int32, (8, 128), 1)
    sub = lax.broadcasted_iota(jnp.int32, (8, 128), 0)
    first_lane = lane == 0
    last_lane = lane == 127
    low_half = lane < 64
    slot16 = lane // 8
    in8 = lane % 8
    c_lo = in8 < 4
    stage2 = stage.reshape(2, VARS * LEV * ROWS, 128)
    ostage2 = ostage.reshape(OVARS * OLEV * OROWS, 128)
    outst2 = outst.reshape(2, VARS * LEV * ROWS, 128)
    oout2 = oout.reshape(OVARS * OLEV * OROWS, 128)
    fout2 = fout.reshape(8 * OROWS, 128)

    def pick(ref, g, t, j):
        return ref[t, pl.ds(g * 8 * ROWS + j, 8, stride=ROWS), :]

    def transpose_group(g, put_left, put_right):
        for half in range(2):
            pack_l = pack_r = None
            for q in range(16):
                j = 16 * half + q
                x0 = pick(stage2, g, 0, j)
                x1 = pick(stage2, g, 1, j)
                a0[g, ASWEEPS + j, 0] = x0
                a0[g, ASWEEPS + j, 1] = x1
                y0 = x0 if q == 0 else pltpu.roll(x0, 8 * q, 1)
                y1 = x1 if q == 15 else pltpu.roll(x1, 8 * q + 8, 1)
                if q == 0:
                    pack_l, pack_r = y0, y1
                else:
                    here = slot16 == q
                    pack_l = jnp.where(here, y0, pack_l)
                    pack_r = jnp.where(here, y1, pack_r)
            put_left(half, pack_l)
            put_right(half, pack_r)

    sends = {}

    def send(src, dst, sem, a, b):
        c = pltpu.make_async_remote_copy(
            src_ref=src,
            dst_ref=dst,
            send_sem=hs_sem.at[sem],
            recv_sem=hr_sem.at[sem],
            device_id={"gx": a, "gy": b},
            device_id_type=MESH,
        )
        c.start()
        sends[sem] = c

    for n in (0, 1):
        for c in ins[n]:
            c.wait()

    def put_gsl(half, x):
        gsl[half] = x

    def put_gsr(half, x):
        gsr[half] = x

    transpose_group(0, put_gsl, put_gsr)
    pl.semaphore_wait(barrier, 8 + GX - 3)

    top_rows = pl.ds(0, ASWEEPS)
    own_first = pl.ds(ASWEEPS, ASWEEPS)
    own_last = pl.ds(ROWS, ASWEEPS)
    bot_rows = pl.ds(ROWS + ASWEEPS, ASWEEPS)
    two = pl.ds(0, 2)
    send(a0.at[0, own_last, two], a0.at[0, top_rows, two], G0_TOP, gx, down)
    send(a0.at[0, own_first, two], a0.at[0, bot_rows, two], G0_BOT, gx, up)
    send(gsl, grr.at[pl.ds(1, 2)], G0_RIGHT, left, gy)
    send(gsr, grl.at[pl.ds(1, 2)], G0_LEFT, right, gy)
    send(gsl.at[pl.ds(1, 1)], grr.at[pl.ds(0, 1)], G0_DIAG, left, down)
    send(gsl.at[pl.ds(0, 1)], grr.at[pl.ds(3, 1)], G0_DIAG + 1, left, up)
    send(gsr.at[pl.ds(1, 1)], grl.at[pl.ds(0, 1)], G0_DIAG + 2, right, down)
    send(gsr.at[pl.ds(0, 1)], grl.at[pl.ds(3, 1)], G0_DIAG + 3, right, up)

    for n in (2, 3, 4):
        for c in ins[n]:
            c.wait()
    for g in (1, 2):

        def put_sl(half, x, g=g):
            sl[(22 if half else 0) + g - 1] = x

        def put_sr(half, x, g=g):
            sr[(22 if half else 0) + g - 1] = x

        transpose_group(g, put_sl, put_sr)

    mcopy.wait()
    wet = maskv[...].astype(jnp.float32)
    for ref in (sl, sr):
        for at in (2, 20):
            ref[at] = wet[0:8]
            ref[at + 1] = wet[8:16]
    su[0] = wet[0:8]
    su[1] = wet[8:16]
    sd[6] = wet[0:8]
    sd[7] = wet[8:16]
    ocopy.wait()
    for j in range(OROWS):
        x = [ostage2[pl.ds(t * OLEV * OROWS + j, 8, stride=OROWS), :] for t in range(2)]
        for t in range(2):
            c0[OSWEEPS + j, t] = x[t]
            if j < OSWEEPS:
                su[2 + 2 * j + t] = x[t]
            if j >= OROWS - OSWEEPS:
                sd[2 * (j - OROWS + OSWEEPS) + t] = x[t]
        sl[4 + j] = jnp.where(c_lo, x[0], pltpu.roll(x[1], 4, 1))
        sr[4 + j] = jnp.where(c_lo, pltpu.roll(x[1], 124, 1), x[0])

    rest = pl.ds(1, 2)
    send(sl, rr.at[pl.ds(7, 24)], SIDE_RIGHT, left, gy)
    send(sr, rl.at[pl.ds(7, 24)], SIDE_LEFT, right, gy)
    send(a0.at[rest, own_last, two], a0.at[rest, top_rows, two], GR_TOP, gx, down)
    send(a0.at[rest, own_first, two], a0.at[rest, bot_rows, two], GR_BOT, gx, up)
    send(sl.at[pl.ds(17, 7)], rr.at[pl.ds(0, 7)], SIDE_DIAG, left, down)
    send(sl.at[pl.ds(0, 7)], rr.at[pl.ds(31, 7)], SIDE_DIAG + 1, left, up)
    send(sr.at[pl.ds(17, 7)], rl.at[pl.ds(0, 7)], SIDE_DIAG + 2, right, down)
    send(sr.at[pl.ds(0, 7)], rl.at[pl.ds(31, 7)], SIDE_DIAG + 3, right, up)
    send(sd, ru, OC_TOP, gx, down)
    send(su, rd, OC_BOT, gx, up)

    rcopy.wait()
    hot_c, hot_j = [], []
    rows16 = lax.broadcasted_iota(jnp.int32, (OROWS, 128), 0)
    for s in range(GX):
        cell = rmap[s : s + 1, :]
        used = lane < rcnt[0, s]
        hot_c.append(jnp.where((cell % 8 == sub) & used, 1.0, 0.0))
        hot_j.append(jnp.where(cell // 128 == rows16, 1.0, 0.0))
    hot_c = jnp.concatenate(hot_c, axis=0).astype(jnp.bfloat16)
    hot_j = jnp.concatenate(hot_j, axis=0).astype(jnp.bfloat16)
    contract = (((1,), (1,)), ((), ()))
    every = lax.dot_general(hot_c, hot_j, contract, preferred_element_type=jnp.float32)
    cell_s = lax.broadcasted_iota(jnp.int32, (OCOLS, GX * OROWS), 0) // 8
    pair_s = lax.broadcasted_iota(jnp.int32, (OCOLS, GX * OROWS), 1) // OROWS
    own = jnp.where(cell_s == pair_s, every, 0.0).astype(jnp.bfloat16)
    fold_j = lax.broadcasted_iota(jnp.int32, (OROWS, GX * OROWS), 0)
    fold_q = lax.broadcasted_iota(jnp.int32, (OROWS, GX * OROWS), 1) % OROWS
    fold = jnp.where(fold_j == fold_q, 1.0, 0.0).astype(jnp.bfloat16)
    live[...] = lax.dot_general(fold, own, contract, preferred_element_type=jnp.float32)

    top_flag = jnp.where(gy == 0, 0.0, 1.0).astype(jnp.float32)
    bot_flag = jnp.where(gy == GY - 1, 0.0, 1.0).astype(jnp.float32)

    def group_kappa(g):
        k = jnp.zeros((8, 128), jnp.float32)
        for p in range(8):
            v, l = ORDER[8 * g + p]
            k = jnp.where(sub == p, kappa[v, l], k)
        return k

    def unpack(g, right_strip, left_strip):
        for i in range(EXT):
            r = i - ASWEEPS + 16
            half, q = r // 16, r % 16
            x = right_strip(half)
            y = left_strip(half)
            x = x if q == 0 else pltpu.roll(x, 128 - 8 * q, 1)
            y = y if q == 15 else pltpu.roll(y, 120 - 8 * q, 1)
            a0[g, i, 2] = jnp.where(low_half, x, y)

        @pl.when(gy == 0)
        def _():
            a0[g, 0:ASWEEPS] = jnp.zeros((ASWEEPS, 3, 8, 128), jnp.float32)

        @pl.when(gy == GY - 1)
        def _():
            a0[g, EXT - ASWEEPS : EXT] = jnp.zeros((ASWEEPS, 3, 8, 128), jnp.float32)

    def rows_step(src, g, i0, n, keep, kap, tiles):
        have = [[src[g, i0 - 1 + q, t] for t in range(3)] for q in range(n + 2)]
        new = []
        for q in range(1, n + 1):
            c, u, d = have[q], have[q - 1], have[q + 1]
            fwd = [pltpu.roll(x, 1, 1) for x in c]
            bwd = [pltpu.roll(x, 127, 1) for x in c]
            line = []
            for t in range(tiles):
                west = jnp.where(first_lane, fwd[(t + 2) % 3], fwd[t])
                east = jnp.where(last_lane, bwd[(t + 1) % 3], bwd[t])
                line.append(keep * c[t] + kap * ((u[t] + d[t]) + (west + east)))
            new.append(line)
        return new

    def sweeps(g, final):
        kap = group_kappa(g)
        keep = 1.0 - 4.0 * kap
        chain = [a0, a1, a2, a1, a2, a1]
        for k in range(1, ASWEEPS):
            src, dst = chain[k - 1], chain[k]

            def put(i0, new, dst=dst):
                for q, line in enumerate(new):
                    for t in range(3):
                        dst[g, i0 + q, t] = line[t]

            n = ASWEEPS - k
            put(k, rows_step(src, g, k, n, keep * top_flag, kap * top_flag, 3))

            def main(b, carry, src=src, put=put):
                i0 = ASWEEPS + 8 * b
                put(i0, rows_step(src, g, i0, 8, keep, kap, 3))
                return carry

            lax.fori_loop(0, ROWS // 8, main, 0)
            i0 = ASWEEPS + ROWS
            put(i0, rows_step(src, g, i0, n, keep * bot_flag, kap * bot_flag, 3))

        def last(b, carry):
            j0 = 8 * b
            new = rows_step(chain[ASWEEPS - 1], g, ASWEEPS + j0, 8, keep, kap, 2)
            for q in range(8):
                for t in range(2):
                    outst2[t, pl.ds(g * 8 * ROWS + j0 + q, 8, stride=ROWS), :] = new[q][t]
            final(b, new)
            return carry

        lax.fori_loop(0, ROWS // 8, last, 0)

    outs = []

    def run_out(n):
        p, v, cnt, l = RUNS[n]
        for t in range(2):
            c = pltpu.make_async_copy(
                outst.at[t, pl.ds(p, cnt)],
                atm_out.at[pl.ds(v, cnt), l, :, pl.ds(128 * t, 128)],
                out_sem.at[2 * n + t],
            )
            c.start()
            outs.append(c)

    for n in range(8):
        sends[n].wait_recv()
    wcopy.wait()
    unpack(0, lambda h: grr[h], lambda h: grl[h])
    even = (2 * lane) % 128

    def coarsen(b, new):
        weights = iw[pl.ds(pl.multiple_of(8 * b, 8), 8), :]
        for q in range(4):
            pair = []
            for t in range(2):
                total = None
                for e in range(2):
                    at = 2 * q + e
                    w = weights[at : at + 1, 128 * t : 128 * t + 128]
                    term = new[2 * q + e][t] * w
                    total = term if total is None else total + term
                total = total + pltpu.roll(total, 127, 1)
                pair.append(
                    jnp.take_along_axis(total, even, axis=1, mode="promise_in_bounds")
                )
            xs[4 * b + q] = jnp.where(low_half, pair[0], pair[1])

    sweeps(0, coarsen)

    def block_transpose(x):
        for bit in (8, 4, 2, 1):
            high = (slot16 // bit) % 2 == 1
            y = list(x)
            for i in range(16):
                if i & bit:
                    continue
                y[i] = jnp.where(high, pltpu.roll(x[i + bit], 8 * bit, 1), x[i])
                y[i + bit] = jnp.where(high, x[i + bit], pltpu.roll(x[i], 128 - 8 * bit, 1))
            x = y
        return x

    for d, x in enumerate(block_transpose([xs[j] for j in range(16)])):
        msg[d] = x

    def remap(k):
        to = lax.rem(gx + k, GX)
        return pltpu.make_async_remote_copy(
            src_ref=msg.at[to],
            dst_ref=got.at[gx],
            send_sem=as_sem.at[k],
            recv_sem=ar_sem.at[gx],
            device_id={"gx": to, "gy": gy},
            device_id_type=MESH,
        )

    moves = [remap(k) for k in range(1, GX)]
    for c in moves:
        c.start()
    got[gx] = msg[gx]
    run_out(0)
    run_out(1)

    for n in (SIDE_RIGHT, SIDE_LEFT, GR_TOP, GR_BOT, *range(SIDE_DIAG, SIDE_DIAG + 4)):
        sends[n].wait_recv()
    for g in (1, 2):
        unpack(g, lambda h, g=g: rr[HALF_AT[h] + g - 1], lambda h, g=g: rl[HALF_AT[h] + g - 1])
        sweeps(g, lambda b, new: None)
        if g == 1:
            run_out(2)
    run_out(3)
    run_out(4)

    for n in (OC_TOP, OC_BOT):
        sends[n].wait_recv()
    for i in range(OSWEEPS):
        for t in range(2):
            c0[i, t] = ru[2 * i + t]
            c0[OSWEEPS + OROWS + i, t] = rd[2 + 2 * i + t]
    wrap_right = jnp.where(gx == GX - 1, 120, 0)
    wrap_left = jnp.where(gx == 0, 8, 0)
    for i in range(OEXT):
        at = i if i < 3 else (i + 8 if i < 19 else i + 16)
        x = pltpu.roll(rr[at], wrap_right, 1)
        y = pltpu.roll(rl[at], wrap_left, 1)
        h0[i, 0] = jnp.where(c_lo, x, y)
        z = jnp.where(c_lo, y, x)
        h0[i, 1] = jnp.where(c_lo, pltpu.roll(z, 124, 1), pltpu.roll(z, 4, 1))
    for part, (at, mid, flag) in enumerate(((3, (ru, 6), top_flag), (9, (su, 0), None), (33, (rd, 0), bot_flag))):
        for e in range(2):
            mc = mid[0][mid[1] + e]
            mh = jnp.where(
                c_lo, pltpu.roll(rr[at + e], wrap_right, 1), pltpu.roll(rl[at + e], wrap_left, 1)
            )
            if flag is not None:
                mc, mh = mc * flag, mh * flag
            mnat[0, pl.ds(16 * part + 8 * e, 8), :] = mc
            mnat[1, pl.ds(16 * part + 8 * e, 8), :] = mh
    for b in range(4):
        r0 = 8 + 8 * b
        m = [mnat[e, r0 : r0 + 8, :] for e in range(2)]
        n = [mnat[e, r0 - 1 : r0 + 7, :] for e in range(2)]
        s = [mnat[e, r0 + 1 : r0 + 9, :] for e in range(2)]
        for e in range(2):
            ke = m[e] * jnp.where(in8 == 7, pltpu.roll(m[1 - e], 7, 1), pltpu.roll(m[e], 127, 1))
            kw = m[e] * jnp.where(in8 == 0, pltpu.roll(m[1 - e], 121, 1), pltpu.roll(m[e], 1, 1))
            kn = m[e] * n[e]
            ks = m[e] * s[e]
            for which, value in enumerate((ke, kw, kn, ks, (ke + kw) + (kn + ks))):
                ko[e, which, pl.ds(8 * b, 8), :] = value

    okap = []
    for t in range(2):
        k = jnp.zeros((8, 128), jnp.float32)
        for l in range(OLEV):
            k = jnp.where(sub == l, okappa[t, l], k)
        okap.append(k)
    levels = [(c0, h0), (c1, h1), (c2, h2)]
    for k in range(1, OSWEEPS + 1):
        src = levels[k - 1]
        final = k == OSWEEPS

        def step(i, carry, src=src, final=final, k=k):
            for e in range(1 if final else 2):
                co = [ko[e, w, pl.ds(i + 5, 1), :] for w in range(5)]
                for t in range(2):
                    me, other = src[e], src[1 - e]
                    o, x = me[i, t], other[i, t]
                    east = jnp.where(in8 == 7, pltpu.roll(x, 7, 1), pltpu.roll(o, 127, 1))
                    west = jnp.where(in8 == 0, pltpu.roll(x, 121, 1), pltpu.roll(o, 1, 1))
                    flux = (co[0] * east + co[1] * west) + (
                        co[2] * me[i - 1, t] + co[3] * me[i + 1, t]
                    )
                    new = o + okap[t] * (flux - co[4] * o)
                    if final:
                        oout2[pl.ds(t * OLEV * OROWS + i - OSWEEPS, 8, stride=OROWS), :] = new
                    else:
                        levels[k][e][i, t] = new
            return carry

        lax.fori_loop(k, OEXT - k, step, 0)

    deep = pltpu.make_async_copy(
        oout.at[:, pl.ds(1, OLEV - 1)], oce_out.at[:, pl.ds(1, OLEV - 1)], out_sem.at[10]
    )
    deep.start()

    for k in range(1, GX):
        frm = lax.rem(gx + k, GX)
        pltpu.make_async_remote_copy(
            src_ref=msg.at[frm],
            dst_ref=got.at[frm],
            send_sem=as_sem.at[k],
            recv_sem=ar_sem.at[frm],
            device_id={"gx": frm, "gy": gy},
            device_id_type=MESH,
        ).wait_recv()
    for j, x in enumerate(block_transpose([got[s] for s in range(16)])):
        fout2[pl.ds(j, 8, stride=OROWS), :] = x * live[j : j + 1, :]
    fcopy = pltpu.make_async_copy(fout.at[pl.ds(0, VARS)], forc_out, out_sem.at[11])
    fcopy.start()
    wet = maskv[...].astype(jnp.float32)
    for t in range(2):
        pushed = None
        for f in range(VARS):
            term = gain[t, f] * fout[f]
            pushed = term if pushed is None else pushed + term
        oout[t, 0] = oout[t, 0] + wet * pushed
    shallow = pltpu.make_async_copy(
        oout.at[:, pl.ds(0, 1)], oce_out.at[:, pl.ds(0, 1)], out_sem.at[12]
    )
    shallow.start()
    for c in sends.values():
        c.wait_send()
    for c in moves:
        c.wait_send()
    for c in outs + [deep, fcopy, shallow]:
        c.wait()


def per_device(
    atm_state,
    atm_kappa,
    intersection_weight,
    ocean_state,
    ocean_kappa,
    land_mask,
    coupling_gain,
    send_map,
    recv_map,
    recv_count,
):
    f32 = jnp.float32
    smem = pl.BlockSpec(memory_space=pltpu.SMEM)
    hbm = pl.BlockSpec(memory_space=pl.ANY)
    vm = pltpu.VMEM
    v = (8, 128)
    return pl.pallas_call(
        body,
        out_shape=(
            jax.ShapeDtypeStruct((VARS, LEV, ROWS, COLS), f32),
            jax.ShapeDtypeStruct((VARS, OROWS, OCOLS), f32),
            jax.ShapeDtypeStruct((OVARS, OLEV, OROWS, OCOLS), f32),
        ),
        in_specs=[smem] * 4 + [hbm] * 5,
        out_specs=(hbm, hbm, hbm),
        scratch_shapes=[
            vm((2, VARS * LEV, ROWS, 128), f32),
            vm((OVARS, OLEV, OROWS, OCOLS), f32),
            vm((ROWS, COLS), f32),
            vm((OROWS, OCOLS), jnp.int32),
            vm((GX, 128), jnp.int32),
            vm((3, EXT, 3) + v, f32),
            vm((3, EXT, 3) + v, f32),
            vm((3, EXT, 3) + v, f32),
            vm((2,) + v, f32), vm((2,) + v, f32), vm((4,) + v, f32), vm((4,) + v, f32),
            vm((24,) + v, f32), vm((24,) + v, f32), vm((38,) + v, f32), vm((38,) + v, f32),
            vm((8,) + v, f32), vm((8,) + v, f32), vm((8,) + v, f32), vm((8,) + v, f32),
            vm((OEXT, 2) + v, f32), vm((OEXT, 2) + v, f32),
            vm((OEXT, 2) + v, f32), vm((OEXT, 2) + v, f32),
            vm((OEXT, 2) + v, f32), vm((OEXT, 2) + v, f32),
            vm((2, 48, 128), f32),
            vm((2, 5, 32, 128), f32),
            vm((OROWS, OCOLS), f32),
            vm((16,) + v, f32), vm((16,) + v, f32), vm((16,) + v, f32),
            vm((2, VARS * LEV, ROWS, 128), f32),
            vm((OVARS, OLEV, OROWS, OCOLS), f32),
            vm((8, OROWS, OCOLS), f32),
            pltpu.SemaphoreType.DMA((14,)),
            pltpu.SemaphoreType.DMA((13,)),
            pltpu.SemaphoreType.DMA((N_HALO,)),
            pltpu.SemaphoreType.DMA((N_HALO,)),
            pltpu.SemaphoreType.DMA((GX,)),
            pltpu.SemaphoreType.DMA((GX,)),
        ],
        compiler_params=pltpu.CompilerParams(
            collective_id=0, has_side_effects=True, vmem_limit_bytes=32 * 1024 * 1024
        ),
    )(
        atm_kappa,
        ocean_kappa,
        coupling_gain,
        recv_count.reshape(1, GX),
        atm_state,
        intersection_weight,
        ocean_state,
        land_mask,
        recv_map.reshape(GX, 128),
    )


def solution(mesh):
    in_specs = (
        P(None, None, "gy", "gx"),
        P(),
        P("gy", "gx"),
        P(None, None, "gy", "gx"),
        P(),
        P("gy", "gx"),
        P(),
        P("gy", "gx", None, None),
        P("gy", "gx", None, None),
        P("gy", "gx", None),
    )
    out_specs = (P(None, None, "gy", "gx"), P(None, "gy", "gx"), P(None, None, "gy", "gx"))
    return jax.shard_map(
        per_device, mesh=mesh, in_specs=in_specs, out_specs=out_specs, check_vma=False
    )
```

time: 340 us -> 39.8 us (0.12)
  the two profiles are of different devices: /device:TPU:0 before, /device:TPU:1 now
where the time goes in v1:
time: 39.8 us; the launch traced here: 39.4 us
  Pallas kernels  31.6 us (79%)
  local copies, waits for them, and re-layouts  7.12 us (18%)
  between operations  0.68 us (2%)
    pallas_call x1, Pallas kernels, per_device(): pl.pallas_call(body, out_shape=(jax.ShapeDtypeStruct((VARS, LEV, ROWS, CO...  31.6 us
    unnamed x20, local copies, waits for them, and re-layouts  7.12 us

profile of v1, /device:TPU:1, one launch (start us, length us, event | category | flops | bytes accessed | tf_op | source)
XLA Modules:
  0.0 39.4 jit_solution(16664748394234245051)
XLA Ops:
  0.6 0.0 copy-start.3
  0.6 0.0 copy-start.5
  0.7 0.0 copy-start.7
  0.7 0.8 %copy.12.kappa = f32[6,4]{1,0:T(8,128)S(1)} copy(f32[6,4]{0,1:T(4,128)} %param.11) | data formatting | bytes 192 | tf_op args[1]
  1.4 0.0 copy-done.3
  1.4 0.0 copy-done.5
  1.5 0.0 copy-done.7
  1.5 0.0 copy-start
  1.5 1.1 %copy-done = f32[6,4,32,256]{3,2,1,0:T(8,128)S(1)} copy-done((f32[6,4,32,256]{3,2,1,0:T(8,128)S(1)}, f32[6,4,32,256]{3,2,1,0:T(8,128)}, u32[]{:S(2)}) %copy-start) | copy-done | bytes 786456
  2.6 0.0 copy-start.1
  2.6 0.9 %copy-done.1 = f32[2,8,16,128]{3,2,1,0:T(8,128)S(1)} copy-done((f32[2,8,16,128]{3,2,1,0:T(8,128)S(1)}, f32[2,8,16,128]{3,2,1,0:T(8,128)}, u32[]{:S(2)}) %copy-start.1) | copy-done | bytes 131096
  3.5 0.0 copy-start.2
  3.5 0.8 %copy-done.2 = f32[32,256]{1,0:T(8,128)S(1)} copy-done((f32[32,256]{1,0:T(8,128)S(1)}, f32[32,256]{1,0:T(8,128)}, u32[]{:S(2)}) %copy-start.2) | copy-done | bytes 32792
  4.3 0.0 copy-start.4
  4.3 0.7 %copy-done.4 = s32[1,1,16,128]{3,2,1,0:T(8,128)S(1)} copy-done((s32[1,1,16,128]{3,2,1,0:T(8,128)S(1)}, s32[1,1,16,128]{3,2,1,0:T(8,128)}, u32[]{:S(2)}) %copy-start.4) | copy-done | bytes 8216
  5.0 0.0 copy-start.6
  5.0 0.7 %copy-done.6 = f32[2,6]{1,0:T(2,128)S(1)} copy-done((f32[2,6]{1,0:T(2,128)S(1)}, f32[2,6]{1,0:T(2,128)}, u32[]{:S(2)}) %copy-start.6) | copy-done | bytes 72
  5.6 31.6 %shard_map.112 = (f32[6,4,32,256]{3,2,1,0:T(8,128)S(1)}, f32[6,16,128]{2,1,0:T(8,128)S(1)}, f32[2,8,16,128]{3,2,1,0:T(8,128)S(1)}) custom-call(f32[6,4]{1,0:T(8,128)S(1)} %copy.12.kappa, f32[2,8]{1,0:T(2,128)S(1)} %copy-done.5, f32[2,6]{1,0:T(2,128)S(1)} %copy-done.6, s32[1,16]{1,0:T(1,128)S(1)} %bitcast.3, f32[6,4,32,256]{3,2,1,0:T(8,128)S(1)} %copy-done, ...), custom_call_target="tpu_custom_call" | custom-call | tf_op jit(solution)/shard_map/pallas_call | solution.py:523
  37.3 0.9 %copy.16 = f32[6,4,32,256]{3,2,1,0:T(8,128)} copy(f32[6,4,32,256]{3,2,1,0:T(8,128)S(1)} %get-tuple-element.6) | data formatting | bytes 1572864
  38.2 0.6 %copy.17 = f32[6,16,128]{2,1,0:T(8,128)} copy(f32[6,16,128]{2,1,0:T(8,128)S(1)} %get-tuple-element.7) | data formatting | bytes 98304
  38.8 0.7 %copy.18 = f32[2,8,16,128]{3,2,1,0:T(8,128)} copy(f32[2,8,16,128]{3,2,1,0:T(8,128)S(1)} %get-tuple-element.8) | data formatting | bytes 262144
Async XLA Ops:
  0.6 0.8 %copy-start.3 = (s32[16,128]{1,0:T(8,128)S(1)}, s32[16,128]{1,0:T(8,128)}, u32[]{:S(2)}) copy-start(s32[16,128]{1,0:T(8,128)} %mask_in.1) | copy-start | bytes 24580
  0.6 0.8 %copy-start.5 = (f32[2,8]{1,0:T(2,128)S(1)}, f32[2,8]{1,0:T(2,128)}, u32[]{:S(2)}) copy-start(f32[2,8]{1,0:T(2,128)} %okappa.1) | copy-start | bytes 196
  0.7 0.8 %copy-start.7 = (s32[1,1,16]{2,1,0:T(1,128)S(1)}, s32[1,1,16]{2,1,0:T(1,128)}, u32[]{:S(2)}) copy-start(s32[1,1,16]{2,1,0:T(1,128)} %param.18) | copy-start | bytes 196
  1.5 1.1 %copy-start = (f32[6,4,32,256]{3,2,1,0:T(8,128)S(1)}, f32[6,4,32,256]{3,2,1,0:T(8,128)}, u32[]{:S(2)}) copy-start(f32[6,4,32,256]{3,2,1,0:T(8,128)} %atm.1) | copy-start | bytes 2359300
  2.6 0.9 %copy-start.1 = (f32[2,8,16,128]{3,2,1,0:T(8,128)S(1)}, f32[2,8,16,128]{3,2,1,0:T(8,128)}, u32[]{:S(2)}) copy-start(f32[2,8,16,128]{3,2,1,0:T(8,128)} %oce.1) | copy-start | bytes 393220
  3.5 0.8 %copy-start.2 = (f32[32,256]{1,0:T(8,128)S(1)}, f32[32,256]{1,0:T(8,128)}, u32[]{:S(2)}) copy-start(f32[32,256]{1,0:T(8,128)} %iw_in.1) | copy-start | bytes 98308
  4.3 0.7 %copy-start.4 = (s32[1,1,16,128]{3,2,1,0:T(8,128)S(1)}, s32[1,1,16,128]{3,2,1,0:T(8,128)}, u32[]{:S(2)}) copy-start(s32[1,1,16,128]{3,2,1,0:T(8,128)} %param.17) | copy-start | bytes 24580
  5.0 0.7 %copy-start.6 = (f32[2,6]{1,0:T(2,128)S(1)}, f32[2,6]{1,0:T(2,128)}, u32[]{:S(2)}) copy-start(f32[2,6]{1,0:T(2,128)} %gain.1) | copy-start | bytes 148

commit v2 on v1

--- a/solution.py
+++ b/solution.py
@@ -34,7 +34,7 @@
 def body(
     kappa, okappa, gain, rcnt,
     atm, iw_in, oce, mask_in, rmap_in,
-    atm_out, forc_out, oce_out,
+    outst, fout, oout,
     stage, ostage, iw, maskv, rmap,
     a0, a1, a2,
     gsl, gsr, grr, grl,
@@ -43,8 +43,7 @@
     c0, h0, c1, h1, c2, h2,
     mnat, ko, live,
     xs, msg, got,
-    outst, oout, fout,
-    in_sem, out_sem, hs_sem, hr_sem, as_sem, ar_sem,
+    in_sem, hs_sem, hr_sem, as_sem, ar_sem,
 ):
     gx = lax.axis_index("gx")
     gy = lax.axis_index("gy")
@@ -244,7 +243,7 @@
         k = jnp.zeros((8, 128), jnp.float32)
         for p in range(8):
             v, l = ORDER[8 * g + p]
-            k = jnp.where(sub == p, kappa[v, l], k)
+            k = jnp.where(sub == p, kappa[l, v], k)
         return k
 
     def unpack(g, right_strip, left_strip):
@@ -300,7 +299,7 @@
                 put(i0, rows_step(src, g, i0, 8, keep, kap, 3))
                 return carry
 
-            lax.fori_loop(0, ROWS // 8, main, 0)
+            lax.fori_loop(0, ROWS // 8, main, 0, unroll=True)
             i0 = ASWEEPS + ROWS
             put(i0, rows_step(src, g, i0, n, keep * bot_flag, kap * bot_flag, 3))
 
@@ -313,20 +312,7 @@
             final(b, new)
             return carry
 
-        lax.fori_loop(0, ROWS // 8, last, 0)
-
-    outs = []
-
-    def run_out(n):
-        p, v, cnt, l = RUNS[n]
-        for t in range(2):
-            c = pltpu.make_async_copy(
-                outst.at[t, pl.ds(p, cnt)],
-                atm_out.at[pl.ds(v, cnt), l, :, pl.ds(128 * t, 128)],
-                out_sem.at[2 * n + t],
-            )
-            c.start()
-            outs.append(c)
+        lax.fori_loop(0, ROWS // 8, last, 0, unroll=True)
 
     for n in range(8):
         sends[n].wait_recv()
@@ -335,7 +321,7 @@
     even = (2 * lane) % 128
 
     def coarsen(b, new):
-        weights = iw[pl.ds(pl.multiple_of(8 * b, 8), 8), :]
+        weights = iw[pl.ds(8 * b, 8), :]
         for q in range(4):
             pair = []
             for t in range(2):
@@ -383,18 +369,12 @@
     for c in moves:
         c.start()
     got[gx] = msg[gx]
-    run_out(0)
-    run_out(1)
 
     for n in (SIDE_RIGHT, SIDE_LEFT, GR_TOP, GR_BOT, *range(SIDE_DIAG, SIDE_DIAG + 4)):
         sends[n].wait_recv()
     for g in (1, 2):
         unpack(g, lambda h, g=g: rr[HALF_AT[h] + g - 1], lambda h, g=g: rl[HALF_AT[h] + g - 1])
         sweeps(g, lambda b, new: None)
-        if g == 1:
-            run_out(2)
-    run_out(3)
-    run_out(4)
 
     for n in (OC_TOP, OC_BOT):
         sends[n].wait_recv()
@@ -465,11 +445,6 @@
 
         lax.fori_loop(k, OEXT - k, step, 0)
 
-    deep = pltpu.make_async_copy(
-        oout.at[:, pl.ds(1, OLEV - 1)], oce_out.at[:, pl.ds(1, OLEV - 1)], out_sem.at[10]
-    )
-    deep.start()
-
     for k in range(1, GX):
         frm = lax.rem(gx + k, GX)
         pltpu.make_async_remote_copy(
@@ -482,8 +457,6 @@
         ).wait_recv()
     for j, x in enumerate(block_transpose([got[s] for s in range(16)])):
         fout2[pl.ds(j, 8, stride=OROWS), :] = x * live[j : j + 1, :]
-    fcopy = pltpu.make_async_copy(fout.at[pl.ds(0, VARS)], forc_out, out_sem.at[11])
-    fcopy.start()
     wet = maskv[...].astype(jnp.float32)
     for t in range(2):
         pushed = None
@@ -491,15 +464,27 @@
             term = gain[t, f] * fout[f]
             pushed = term if pushed is None else pushed + term
         oout[t, 0] = oout[t, 0] + wet * pushed
-    shallow = pltpu.make_async_copy(
-        oout.at[:, pl.ds(0, 1)], oce_out.at[:, pl.ds(0, 1)], out_sem.at[12]
-    )
-    shallow.start()
     for c in sends.values():
         c.wait_send()
     for c in moves:
         c.wait_send()
-    for c in outs + [deep, fcopy, shallow]:
+
+
+def write_out(outst, fout, oout, atm_out, forc_out, oce_out, sem):
+    copies = [
+        pltpu.make_async_copy(
+            outst.at[t, pl.ds(p, cnt)],
+            atm_out.at[pl.ds(v, cnt), l, :, pl.ds(128 * t, 128)],
+            sem.at[2 * n + t],
+        )
+        for n, (p, v, cnt, l) in enumerate(RUNS)
+        for t in range(2)
+    ]
+    copies.append(pltpu.make_async_copy(oout, oce_out, sem.at[10]))
+    copies.append(pltpu.make_async_copy(fout.at[pl.ds(0, VARS)], forc_out, sem.at[11]))
+    for c in copies:
+        c.start()
+    for c in copies:
         c.wait()
 
 
@@ -520,15 +505,25 @@
     hbm = pl.BlockSpec(memory_space=pl.ANY)
     vm = pltpu.VMEM
     v = (8, 128)
-    return pl.pallas_call(
+    staged = (
+        (2, VARS * LEV, ROWS, 128),
+        (8, OROWS, OCOLS),
+        (OVARS, OLEV, OROWS, OCOLS),
+    )
+    shapes = (
+        (VARS, LEV, ROWS, COLS),
+        (VARS, OROWS, OCOLS),
+        (OVARS, OLEV, OROWS, OCOLS),
+    )
+
+    def in_hbm(x):
+        return pltpu.with_memory_space_constraint(x, pltpu.HBM)
+
+    done = pl.pallas_call(
         body,
-        out_shape=(
-            jax.ShapeDtypeStruct((VARS, LEV, ROWS, COLS), f32),
-            jax.ShapeDtypeStruct((VARS, OROWS, OCOLS), f32),
-            jax.ShapeDtypeStruct((OVARS, OLEV, OROWS, OCOLS), f32),
-        ),
+        out_shape=tuple(pltpu.VMEM(shape, f32) for shape in staged),
         in_specs=[smem] * 4 + [hbm] * 5,
-        out_specs=(hbm, hbm, hbm),
+        out_specs=(pl.BlockSpec(memory_space=pltpu.VMEM),) * 3,
         scratch_shapes=[
             vm((2, VARS * LEV, ROWS, 128), f32),
             vm((OVARS, OLEV, OROWS, OCOLS), f32),
@@ -548,11 +543,7 @@
             vm((2, 5, 32, 128), f32),
             vm((OROWS, OCOLS), f32),
             vm((16,) + v, f32), vm((16,) + v, f32), vm((16,) + v, f32),
-            vm((2, VARS * LEV, ROWS, 128), f32),
-            vm((OVARS, OLEV, OROWS, OCOLS), f32),
-            vm((8, OROWS, OCOLS), f32),
             pltpu.SemaphoreType.DMA((14,)),
-            pltpu.SemaphoreType.DMA((13,)),
             pltpu.SemaphoreType.DMA((N_HALO,)),
             pltpu.SemaphoreType.DMA((N_HALO,)),
             pltpu.SemaphoreType.DMA((GX,)),
@@ -562,16 +553,24 @@
             collective_id=0, has_side_effects=True, vmem_limit_bytes=32 * 1024 * 1024
         ),
     )(
-        atm_kappa,
-        ocean_kappa,
-        coupling_gain,
-        recv_count.reshape(1, GX),
-        atm_state,
-        intersection_weight,
-        ocean_state,
-        land_mask,
-        recv_map.reshape(GX, 128),
+        in_hbm(atm_kappa.T),
+        in_hbm(ocean_kappa),
+        in_hbm(coupling_gain),
+        in_hbm(recv_count.reshape(1, GX)),
+        in_hbm(atm_state),
+        in_hbm(intersection_weight),
+        in_hbm(ocean_state),
+        in_hbm(land_mask),
+        in_hbm(recv_map.reshape(GX, 128)),
     )
+    return pl.pallas_call(
+        write_out,
+        out_shape=tuple(pltpu.HBM(shape, f32) for shape in shapes),
+        in_specs=[pl.BlockSpec(memory_space=pltpu.VMEM)] * 3,
+        out_specs=(hbm, hbm, hbm),
+        scratch_shapes=[pltpu.SemaphoreType.DMA((12,))],
+        compiler_params=pltpu.CompilerParams(vmem_limit_bytes=4 * 1024 * 1024),
+    )(*(pltpu.with_memory_space_constraint(x, pltpu.VMEM) for x in done))
 
 
 def solution(mesh):

time: 39.8 us -> 26.6 us (0.67)
  local copies, waits for them, and re-layouts: 7.12 us -> 0 us
  Pallas kernels: 31.6 us -> 25.8 us
    unnamed x20 -> x0, local copies, waits for them, and re-layouts: 7.12 us -> none
    pallas_call x1 -> x2, Pallas kernels: 31.6 us -> 25.8 us  [the longest x1 24.8 us: per_device(): pl.pallas_call(body, out_shape=tuple((pltpu.VMEM(shape, f32) for shape in...]
where the time goes in v2:
time: 26.6 us; the launch traced here: 26.4 us
  Pallas kernels  25.8 us (97%)
  between operations  0.64 us (2%)
    pallas_call x1, Pallas kernels, per_device(): pl.pallas_call(body, out_shape=tuple((pltpu.VMEM(shape, f32) for shape in...  24.8 us
    pallas_call x1, Pallas kernels, per_device(): pl.pallas_call(write_out, out_shape=tuple((pltpu.HBM(shape, f32) for shap...  1.03 us

profile of v2, /device:TPU:1, one launch (start us, length us, event | category | flops | bytes accessed | tf_op | source)
XLA Modules:
  0.0 26.4 jit_solution(15089168963608472248)
XLA Ops:
  0.6 24.8 %shard_map.112 = (f32[2,24,32,128]{3,2,1,0:T(8,128)S(1)}, f32[8,16,128]{2,1,0:T(8,128)S(1)}, f32[2,8,16,128]{3,2,1,0:T(8,128)S(1)}) custom-call(f32[4,6]{1,0:T(4,128)} %bitcast.4, f32[2,8]{1,0:T(2,128)} %okappa.1, f32[2,6]{1,0:T(2,128)} %gain.1, s32[1,16]{1,0:T(1,128)} %bitcast.5, f32[6,4,32,256]{3,2,1,0:T(8,128)} %atm.1, f32[32,256]{1,0:T(8,128)} %iw_in.1, ...), custom_call_target="tpu_custom_call" | custom-call | tf_op jit(solution)/shard_map/pallas_call | solution.py:522
  25.4 1.0 %shard_map.113 = (f32[6,4,32,256]{3,2,1,0:T(8,128)}, f32[6,16,128]{2,1,0:T(8,128)}, f32[2,8,16,128]{3,2,1,0:T(8,128)}) custom-call(f32[2,24,32,128]{3,2,1,0:T(8,128)S(1)} %get-tuple-element.6.outst, f32[8,16,128]{2,1,0:T(8,128)S(1)} %get-tuple-element.7.fout, f32[2,8,16,128]{3,2,1,0:T(8,128)S(1)} %get-tuple-element.8.oout), custom_call_target="tpu_custom_call" | custom-call | tf_op jit(solution)/shard_map/pallas_call | solution.py:566

commit v3 on v2

--- a/solution.py
+++ b/solution.py
@@ -32,16 +32,17 @@
 
 
 def body(
-    kappa, okappa, gain, rcnt,
+    kappa_in, okappa_in, gain_in, rcnt_in,
     atm, iw_in, oce, mask_in, rmap_in,
     outst, fout, oout,
+    kappa, okappa, gain, rcnt,
     stage, ostage, iw, maskv, rmap,
     a0, a1, a2,
     gsl, gsr, grr, grl,
     sl, sr, rr, rl,
     su, sd, ru, rd,
     c0, h0, c1, h1, c2, h2,
-    mnat, ko, live,
+    mnat, ko, live, kvs,
     xs, msg, got,
     in_sem, hs_sem, hr_sem, as_sem, ar_sem,
 ):
@@ -69,6 +70,12 @@
     wcopy = pltpu.make_async_copy(iw_in, iw, in_sem.at[11])
     mcopy = pltpu.make_async_copy(mask_in, maskv, in_sem.at[12])
     rcopy = pltpu.make_async_copy(rmap_in, rmap, in_sem.at[13])
+    scalars = [
+        pltpu.make_async_copy(src, dst, in_sem.at[14 + n])
+        for n, (src, dst) in enumerate(
+            ((kappa_in, kappa), (okappa_in, okappa), (gain_in, gain), (rcnt_in, rcnt))
+        )
+    ]
 
     barrier = pltpu.get_barrier_semaphore()
 
@@ -88,7 +95,7 @@
     for n in (2, 3, 4):
         for c in ins[n]:
             c.start()
-    for c in (ocopy, mcopy, wcopy, rcopy):
+    for c in (ocopy, mcopy, wcopy, rcopy, *scalars):
         c.start()
 
     lane = lax.broadcasted_iota(jnp.int32, (8, 128), 1)
@@ -217,6 +224,8 @@
     send(su, rd, OC_BOT, gx, up)
 
     rcopy.wait()
+    for c in scalars:
+        c.wait()
     hot_c, hot_j = [], []
     rows16 = lax.broadcasted_iota(jnp.int32, (OROWS, 128), 0)
     for s in range(GX):
@@ -280,7 +289,7 @@
         return new
 
     def sweeps(g, final):
-        kap = group_kappa(g)
+        kap = group_kappa(g) if isinstance(g, int) else kvs[g - 1]
         keep = 1.0 - 4.0 * kap
         chain = [a0, a1, a2, a1, a2, a1]
         for k in range(1, ASWEEPS):
@@ -372,9 +381,15 @@
 
     for n in (SIDE_RIGHT, SIDE_LEFT, GR_TOP, GR_BOT, *range(SIDE_DIAG, SIDE_DIAG + 4)):
         sends[n].wait_recv()
-    for g in (1, 2):
+    kvs[0] = group_kappa(1)
+    kvs[1] = group_kappa(2)
+
+    def each(g, carry):
         unpack(g, lambda h, g=g: rr[HALF_AT[h] + g - 1], lambda h, g=g: rl[HALF_AT[h] + g - 1])
         sweeps(g, lambda b, new: None)
+        return carry
+
+    lax.fori_loop(1, 3, each, 0)
 
     for n in (OC_TOP, OC_BOT):
         sends[n].wait_recv()
@@ -425,7 +440,7 @@
         src = levels[k - 1]
         final = k == OSWEEPS
 
-        def step(i, carry, src=src, final=final, k=k):
+        def step(i, src=src, final=final, k=k):
             for e in range(1 if final else 2):
                 co = [ko[e, w, pl.ds(i + 5, 1), :] for w in range(5)]
                 for t in range(2):
@@ -441,9 +456,9 @@
                         oout2[pl.ds(t * OLEV * OROWS + i - OSWEEPS, 8, stride=OROWS), :] = new
                     else:
                         levels[k][e][i, t] = new
-            return carry
-
-        lax.fori_loop(k, OEXT - k, step, 0)
+
+        for i in range(k, OEXT - k):
+            step(i)
 
     for k in range(1, GX):
         frm = lax.rem(gx + k, GX)
@@ -501,7 +516,7 @@
     recv_count,
 ):
     f32 = jnp.float32
-    smem = pl.BlockSpec(memory_space=pltpu.SMEM)
+    sm = pltpu.SMEM
     hbm = pl.BlockSpec(memory_space=pl.ANY)
     vm = pltpu.VMEM
     v = (8, 128)
@@ -522,9 +537,10 @@
     done = pl.pallas_call(
         body,
         out_shape=tuple(pltpu.VMEM(shape, f32) for shape in staged),
-        in_specs=[smem] * 4 + [hbm] * 5,
+        in_specs=[hbm] * 9,
         out_specs=(pl.BlockSpec(memory_space=pltpu.VMEM),) * 3,
         scratch_shapes=[
+            sm((LEV, VARS), f32), sm((OVARS, OLEV), f32), sm((OVARS, VARS), f32), sm((1, GX), jnp.int32),
             vm((2, VARS * LEV, ROWS, 128), f32),
             vm((OVARS, OLEV, OROWS, OCOLS), f32),
             vm((ROWS, COLS), f32),
@@ -542,8 +558,9 @@
             vm((2, 48, 128), f32),
             vm((2, 5, 32, 128), f32),
             vm((OROWS, OCOLS), f32),
+            vm((2,) + v, f32),
             vm((16,) + v, f32), vm((16,) + v, f32), vm((16,) + v, f32),
-            pltpu.SemaphoreType.DMA((14,)),
+            pltpu.SemaphoreType.DMA((18,)),
             pltpu.SemaphoreType.DMA((N_HALO,)),
             pltpu.SemaphoreType.DMA((N_HALO,)),
             pltpu.SemaphoreType.DMA((GX,)),

time: 26.6 us -> 22.6 us (0.85)
  Pallas kernels: 25.8 us -> 21.9 us
    pallas_call x1, Pallas kernels: 24.8 us -> 20.8 us  [per_device(): pl.pallas_call(body, out_shape=tuple((pltpu.VMEM(shape, f32) for shape in...]
where the time goes in v3:
time: 22.6 us; the launch traced here: 22.5 us
  Pallas kernels  21.9 us (97%)
  between operations  0.64 us (3%)
    pallas_call x1, Pallas kernels, per_device(): pl.pallas_call(body, out_shape=tuple((pltpu.VMEM(shape, f32) for shape in...  20.8 us
    pallas_call x1, Pallas kernels, per_device(): pl.pallas_call(write_out, out_shape=tuple((pltpu.HBM(shape, f32) for shap...  1.03 us

profile of v3, /device:TPU:1, one launch (start us, length us, event | category | flops | bytes accessed | tf_op | source)
XLA Modules:
  0.0 22.5 jit_solution(2083693573988502589)
XLA Ops:
  0.6 20.8 %shard_map.112 = (f32[2,24,32,128]{3,2,1,0:T(8,128)S(1)}, f32[8,16,128]{2,1,0:T(8,128)S(1)}, f32[2,8,16,128]{3,2,1,0:T(8,128)S(1)}) custom-call(f32[4,6]{1,0:T(4,128)} %bitcast.4, f32[2,8]{1,0:T(2,128)} %okappa_in.1, f32[2,6]{1,0:T(2,128)} %gain_in.1, s32[1,16]{1,0:T(1,128)} %bitcast.5, f32[6,4,32,256]{3,2,1,0:T(8,128)} %atm.1, f32[32,256]{1,0:T(8,128)} %iw_in.1, ...), custom_call_target="tpu_custom_call" | custom-call | tf_op jit(solution)/shard_map/pallas_call | solution.py:537
  21.5 1.0 %shard_map.113 = (f32[6,4,32,256]{3,2,1,0:T(8,128)}, f32[6,16,128]{2,1,0:T(8,128)}, f32[2,8,16,128]{3,2,1,0:T(8,128)}) custom-call(f32[2,24,32,128]{3,2,1,0:T(8,128)S(1)} %get-tuple-element.6.outst, f32[8,16,128]{2,1,0:T(8,128)S(1)} %get-tuple-element.7.fout, f32[2,8,16,128]{3,2,1,0:T(8,128)S(1)} %get-tuple-element.8.oout), custom_call_target="tpu_custom_call" | custom-call | tf_op jit(solution)/shard_map/pallas_call | solution.py:583

commit v4 on v3

--- a/solution.py
+++ b/solution.py
@@ -14,6 +14,7 @@
 OROWS, OCOLS = 16, 128
 EXT = ROWS + 2 * ASWEEPS
 OEXT = OROWS + 2 * OSWEEPS
+BAND = 16 + 2 * ASWEEPS
 MESH = pl.DeviceIdType.MESH
 
 ORDER = (
@@ -37,12 +38,12 @@
     outst, fout, oout,
     kappa, okappa, gain, rcnt,
     stage, ostage, iw, maskv, rmap,
-    a0, a1, a2,
+    tt, s0, s12, own0, own12,
     gsl, gsr, grr, grl,
     sl, sr, rr, rl,
     su, sd, ru, rd,
     c0, h0, c1, h1, c2, h2,
-    mnat, ko, live, kvs,
+    mnat, ko, live,
     xs, msg, got,
     in_sem, hs_sem, hr_sem, as_sem, ar_sem,
 ):
@@ -84,11 +85,11 @@
             barrier, inc=1, device_id={"gx": a, "gy": b}, device_id_type=MESH
         )
 
-    for a in (left, gx, right):
-        for b in (up, gy, down):
-            if a is gx and b is gy:
-                continue
+    for a in (left, right):
+        for b in (up, down):
             greet(a, b)
+    for a, b in ((left, gy), (right, gy), (gx, up), (gx, down)):
+        greet(a, b)
     for k in range(2, GX - 1):
         greet(lax.rem(gx + k, GX), gy)
 
@@ -115,6 +116,28 @@
     def pick(ref, g, t, j):
         return ref[t, pl.ds(g * 8 * ROWS + j, 8, stride=ROWS), :]
 
+    strip_right = lane % 64 >= 32
+
+    def own_strip(x0, x1, base):
+        y0 = pltpu.roll(x0, base + 8, 1)
+        y1 = pltpu.roll(x1, (base + 56) % 128, 1)
+        return jnp.where(strip_right, y1, y0)
+
+    def put_own(g, r, x0, x1):
+        if g == 0:
+            if r < 16 + ASWEEPS:
+                own0[r + ASWEEPS] = own_strip(x0, x1, 0)
+            if r >= 16 - ASWEEPS:
+                m = r - 16 + ASWEEPS
+                y = own_strip(x0, x1, 64)
+                own0[m] = y if m < ASWEEPS else jnp.where(low_half, own0[m], y)
+        elif g == 1:
+            own12[r + ASWEEPS] = own_strip(x0, x1, 0)
+        else:
+            own12[r + ASWEEPS] = jnp.where(
+                low_half, own12[r + ASWEEPS], own_strip(x0, x1, 64)
+            )
+
     def transpose_group(g, put_left, put_right):
         for half in range(2):
             pack_l = pack_r = None
@@ -122,8 +145,9 @@
                 j = 16 * half + q
                 x0 = pick(stage2, g, 0, j)
                 x1 = pick(stage2, g, 1, j)
-                a0[g, ASWEEPS + j, 0] = x0
-                a0[g, ASWEEPS + j, 1] = x1
+                tt[0, g, ASWEEPS + j, 0] = x0
+                tt[0, g, ASWEEPS + j, 1] = x1
+                put_own(g, j, x0, x1)
                 y0 = x0 if q == 0 else pltpu.roll(x0, 8 * q, 1)
                 y1 = x1 if q == 15 else pltpu.roll(x1, 8 * q + 8, 1)
                 if q == 0:
@@ -160,21 +184,10 @@
         gsr[half] = x
 
     transpose_group(0, put_gsl, put_gsr)
-    pl.semaphore_wait(barrier, 8 + GX - 3)
-
     top_rows = pl.ds(0, ASWEEPS)
     own_first = pl.ds(ASWEEPS, ASWEEPS)
     own_last = pl.ds(ROWS, ASWEEPS)
     bot_rows = pl.ds(ROWS + ASWEEPS, ASWEEPS)
-    two = pl.ds(0, 2)
-    send(a0.at[0, own_last, two], a0.at[0, top_rows, two], G0_TOP, gx, down)
-    send(a0.at[0, own_first, two], a0.at[0, bot_rows, two], G0_BOT, gx, up)
-    send(gsl, grr.at[pl.ds(1, 2)], G0_RIGHT, left, gy)
-    send(gsr, grl.at[pl.ds(1, 2)], G0_LEFT, right, gy)
-    send(gsl.at[pl.ds(1, 1)], grr.at[pl.ds(0, 1)], G0_DIAG, left, down)
-    send(gsl.at[pl.ds(0, 1)], grr.at[pl.ds(3, 1)], G0_DIAG + 1, left, up)
-    send(gsr.at[pl.ds(1, 1)], grl.at[pl.ds(0, 1)], G0_DIAG + 2, right, down)
-    send(gsr.at[pl.ds(0, 1)], grl.at[pl.ds(3, 1)], G0_DIAG + 3, right, up)
 
     for n in (2, 3, 4):
         for c in ins[n]:
@@ -211,21 +224,90 @@
         sl[4 + j] = jnp.where(c_lo, x[0], pltpu.roll(x[1], 4, 1))
         sr[4 + j] = jnp.where(c_lo, pltpu.roll(x[1], 124, 1), x[0])
 
-    rest = pl.ds(1, 2)
-    send(sl, rr.at[pl.ds(7, 24)], SIDE_RIGHT, left, gy)
-    send(sr, rl.at[pl.ds(7, 24)], SIDE_LEFT, right, gy)
-    send(a0.at[rest, own_last, two], a0.at[rest, top_rows, two], GR_TOP, gx, down)
-    send(a0.at[rest, own_first, two], a0.at[rest, bot_rows, two], GR_BOT, gx, up)
-    send(sl.at[pl.ds(17, 7)], rr.at[pl.ds(0, 7)], SIDE_DIAG, left, down)
-    send(sl.at[pl.ds(0, 7)], rr.at[pl.ds(31, 7)], SIDE_DIAG + 1, left, up)
-    send(sr.at[pl.ds(17, 7)], rl.at[pl.ds(0, 7)], SIDE_DIAG + 2, right, down)
-    send(sr.at[pl.ds(0, 7)], rl.at[pl.ds(31, 7)], SIDE_DIAG + 3, right, up)
-    send(sd, ru, OC_TOP, gx, down)
-    send(su, rd, OC_BOT, gx, up)
-
-    rcopy.wait()
+    top_flag = jnp.where(gy == 0, 0.0, 1.0).astype(jnp.float32)
+    bot_flag = jnp.where(gy == GY - 1, 0.0, 1.0).astype(jnp.float32)
     for c in scalars:
         c.wait()
+
+    def group_kappa(g):
+        k = jnp.zeros((8, 128), jnp.float32)
+        for p in range(8):
+            v, l = ORDER[8 * g + p]
+            k = jnp.where(sub == p, kappa[l, v], k)
+        return k
+
+    kaps = [group_kappa(g) for g in range(3)]
+    keeps = [1.0 - 4.0 * k for k in kaps]
+    kap12 = jnp.where(low_half, kaps[1], kaps[2])
+    keep12 = 1.0 - 4.0 * kap12
+
+    def tile_rows(g, k, lo, hi, flag=None):
+        keep, kap = keeps[g], kaps[g]
+        if flag is not None:
+            keep, kap = keep * flag, kap * flag
+        for i0 in range(lo, hi, 8):
+            n = min(8, hi - i0)
+            have = [[tt[k - 1, g, i0 - 1 + q, t] for t in range(2)] for q in range(n + 2)]
+            for q in range(1, n + 1):
+                c, u, d = have[q], have[q - 1], have[q + 1]
+                fwd = [pltpu.roll(x, 1, 1) for x in c]
+                bwd = [pltpu.roll(x, 127, 1) for x in c]
+                west = [fwd[0], jnp.where(first_lane, fwd[0], fwd[1])]
+                east = [jnp.where(last_lane, bwd[1], bwd[0]), bwd[1]]
+                for t in range(2):
+                    tt[k, g, i0 + q - 1, t] = keep * c[t] + kap * (
+                        (u[t] + d[t]) + (west[t] + east[t])
+                    )
+
+    def interior(g):
+        for k in range(1, ASWEEPS + 1):
+            tile_rows(g, k, ASWEEPS + k, ASWEEPS + ROWS - k)
+
+    def rim(g, k):
+        top, bot = ASWEEPS, ASWEEPS + ROWS
+        if k < ASWEEPS:
+            tile_rows(g, k, k, top, top_flag)
+            tile_rows(g, k, bot, EXT - k, bot_flag)
+        tile_rows(g, k, top, top + k)
+        tile_rows(g, k, bot - k, bot)
+
+    def clear_outside(g):
+        @pl.when(gy == 0)
+        def _():
+            tt[0, g, 0:ASWEEPS] = jnp.zeros((ASWEEPS, 2, 8, 128), jnp.float32)
+
+        @pl.when(gy == GY - 1)
+        def _():
+            tt[0, g, EXT - ASWEEPS : EXT] = jnp.zeros((ASWEEPS, 2, 8, 128), jnp.float32)
+
+    strip_edge = (slot16 % 8 == 0) | (slot16 % 8 == 7)
+
+    def strip_halo(a, b, c, d, q):
+        z = jnp.where(slot16 == (q + 7) % 16, c, d)
+        z = jnp.where(slot16 == (q + 8) % 16, b, z)
+        z = jnp.where(slot16 == q, a, z)
+        return z if q == 0 else pltpu.roll(z, 128 - 8 * q, 1)
+
+    def strip_rows(ref, k, lo, hi, coef):
+        have = [ref[k - 1, i] for i in range(lo - 1, hi + 1)]
+        for i in range(lo, hi):
+            c, u, d = have[i - lo + 1], have[i - lo], have[i - lo + 2]
+            keep, kap = coef(i)
+            ref[k, i] = keep * c + kap * (
+                (u + d) + (pltpu.roll(c, 1, 1) + pltpu.roll(c, 127, 1))
+            )
+
+    def merged(g, r, strip, base):
+        x0, x1 = tt[ASWEEPS, g, ASWEEPS + r, 0], tt[ASWEEPS, g, ASWEEPS + r, 1]
+        y0 = pltpu.roll(strip, 120 - base, 1)
+        y1 = pltpu.roll(strip, (72 - base) % 128, 1)
+        return [jnp.where(lane < 8, y0, x0), jnp.where(lane >= 120, y1, x1)]
+
+    def store_rows(g, r, new):
+        for t in range(2):
+            outst2[t, pl.ds(g * 8 * ROWS + r, 8, stride=ROWS), :] = new[t]
+
+    rcopy.wait()
     hot_c, hot_j = [], []
     rows16 = lax.broadcasted_iota(jnp.int32, (OROWS, 128), 0)
     for s in range(GX):
@@ -245,88 +327,72 @@
     fold = jnp.where(fold_j == fold_q, 1.0, 0.0).astype(jnp.bfloat16)
     live[...] = lax.dot_general(fold, own, contract, preferred_element_type=jnp.float32)
 
-    top_flag = jnp.where(gy == 0, 0.0, 1.0).astype(jnp.float32)
-    bot_flag = jnp.where(gy == GY - 1, 0.0, 1.0).astype(jnp.float32)
-
-    def group_kappa(g):
-        k = jnp.zeros((8, 128), jnp.float32)
-        for p in range(8):
-            v, l = ORDER[8 * g + p]
-            k = jnp.where(sub == p, kappa[l, v], k)
-        return k
-
-    def unpack(g, right_strip, left_strip):
-        for i in range(EXT):
-            r = i - ASWEEPS + 16
-            half, q = r // 16, r % 16
-            x = right_strip(half)
-            y = left_strip(half)
-            x = x if q == 0 else pltpu.roll(x, 128 - 8 * q, 1)
-            y = y if q == 15 else pltpu.roll(y, 120 - 8 * q, 1)
-            a0[g, i, 2] = jnp.where(low_half, x, y)
-
-        @pl.when(gy == 0)
-        def _():
-            a0[g, 0:ASWEEPS] = jnp.zeros((ASWEEPS, 3, 8, 128), jnp.float32)
-
-        @pl.when(gy == GY - 1)
-        def _():
-            a0[g, EXT - ASWEEPS : EXT] = jnp.zeros((ASWEEPS, 3, 8, 128), jnp.float32)
-
-    def rows_step(src, g, i0, n, keep, kap, tiles):
-        have = [[src[g, i0 - 1 + q, t] for t in range(3)] for q in range(n + 2)]
-        new = []
-        for q in range(1, n + 1):
-            c, u, d = have[q], have[q - 1], have[q + 1]
-            fwd = [pltpu.roll(x, 1, 1) for x in c]
-            bwd = [pltpu.roll(x, 127, 1) for x in c]
-            line = []
-            for t in range(tiles):
-                west = jnp.where(first_lane, fwd[(t + 2) % 3], fwd[t])
-                east = jnp.where(last_lane, bwd[(t + 1) % 3], bwd[t])
-                line.append(keep * c[t] + kap * ((u[t] + d[t]) + (west + east)))
-            new.append(line)
-        return new
-
-    def sweeps(g, final):
-        kap = group_kappa(g) if isinstance(g, int) else kvs[g - 1]
-        keep = 1.0 - 4.0 * kap
-        chain = [a0, a1, a2, a1, a2, a1]
-        for k in range(1, ASWEEPS):
-            src, dst = chain[k - 1], chain[k]
-
-            def put(i0, new, dst=dst):
-                for q, line in enumerate(new):
-                    for t in range(3):
-                        dst[g, i0 + q, t] = line[t]
-
-            n = ASWEEPS - k
-            put(k, rows_step(src, g, k, n, keep * top_flag, kap * top_flag, 3))
-
-            def main(b, carry, src=src, put=put):
-                i0 = ASWEEPS + 8 * b
-                put(i0, rows_step(src, g, i0, 8, keep, kap, 3))
-                return carry
-
-            lax.fori_loop(0, ROWS // 8, main, 0, unroll=True)
-            i0 = ASWEEPS + ROWS
-            put(i0, rows_step(src, g, i0, n, keep * bot_flag, kap * bot_flag, 3))
-
-        def last(b, carry):
-            j0 = 8 * b
-            new = rows_step(chain[ASWEEPS - 1], g, ASWEEPS + j0, 8, keep, kap, 2)
-            for q in range(8):
-                for t in range(2):
-                    outst2[t, pl.ds(g * 8 * ROWS + j0 + q, 8, stride=ROWS), :] = new[q][t]
-            final(b, new)
-            return carry
-
-        lax.fori_loop(0, ROWS // 8, last, 0, unroll=True)
+    interior(0)
+    pl.semaphore_wait(barrier, 8 + GX - 3)
+
+    send(gsl.at[pl.ds(1, 1)], grr.at[pl.ds(0, 1)], G0_DIAG, left, down)
+    send(gsl.at[pl.ds(0, 1)], grr.at[pl.ds(3, 1)], G0_DIAG + 1, left, up)
+    send(gsr.at[pl.ds(1, 1)], grl.at[pl.ds(0, 1)], G0_DIAG + 2, right, down)
+    send(gsr.at[pl.ds(0, 1)], grl.at[pl.ds(3, 1)], G0_DIAG + 3, right, up)
+    send(gsl, grr.at[pl.ds(1, 2)], G0_RIGHT, left, gy)
+    send(gsr, grl.at[pl.ds(1, 2)], G0_LEFT, right, gy)
+    send(tt.at[0, 0, own_last], tt.at[0, 0, top_rows], G0_TOP, gx, down)
+    send(tt.at[0, 0, own_first], tt.at[0, 0, bot_rows], G0_BOT, gx, up)
+
+    rest = pl.ds(1, 2)
+    send(sl, rr.at[pl.ds(7, 24)], SIDE_RIGHT, left, gy)
+    send(sr, rl.at[pl.ds(7, 24)], SIDE_LEFT, right, gy)
+    send(tt.at[0, rest, own_last], tt.at[0, rest, top_rows], GR_TOP, gx, down)
+    send(tt.at[0, rest, own_first], tt.at[0, rest, bot_rows], GR_BOT, gx, up)
+    send(sl.at[pl.ds(17, 7)], rr.at[pl.ds(0, 7)], SIDE_DIAG, left, down)
+    send(sl.at[pl.ds(0, 7)], rr.at[pl.ds(31, 7)], SIDE_DIAG + 1, left, up)
+    send(sr.at[pl.ds(17, 7)], rl.at[pl.ds(0, 7)], SIDE_DIAG + 2, right, down)
+    send(sr.at[pl.ds(0, 7)], rl.at[pl.ds(31, 7)], SIDE_DIAG + 3, right, up)
+    send(sd, ru, OC_TOP, gx, down)
+    send(su, rd, OC_BOT, gx, up)
+
+    interior(1)
+    interior(2)
 
     for n in range(8):
         sends[n].wait_recv()
     wcopy.wait()
-    unpack(0, lambda h: grr[h], lambda h: grl[h])
+    clear_outside(0)
+    low_top = jnp.where(low_half, top_flag, 1.0)
+    high_bot = jnp.where(low_half, 1.0, bot_flag)
+    strips = [
+        [grl[h] for h in range(4)],
+        [pltpu.roll(grl[h], 64, 1) for h in range(4)],
+        [pltpu.roll(grr[h], 56, 1) for h in range(4)],
+        [pltpu.roll(grr[h], 120, 1) for h in range(4)],
+    ]
+    for m in range(BAND):
+        h, q = (m + 10) // 16, (m + 10) % 16
+        z = strip_halo(strips[0][h], strips[1][h + 1], strips[2][h], strips[3][h + 1], q)
+        own = own0[m]
+        if m < ASWEEPS:
+            own = jnp.where(low_half, own_strip(tt[0, 0, m, 0], tt[0, 0, m, 1], 0), own)
+        if m >= BAND - ASWEEPS:
+            own = jnp.where(
+                low_half, own, own_strip(tt[0, 0, m + 16, 0], tt[0, 0, m + 16, 1], 64)
+            )
+        z = jnp.where(strip_edge, z, own)
+        if m < ASWEEPS:
+            z = z * low_top
+        if m >= BAND - ASWEEPS:
+            z = z * high_bot
+        s0[0, m] = z
+
+    def coef0(m):
+        if m < ASWEEPS:
+            return keeps[0] * low_top, kaps[0] * low_top
+        if m >= BAND - ASWEEPS:
+            return keeps[0] * high_bot, kaps[0] * high_bot
+        return keeps[0], kaps[0]
+
+    for k in range(1, ASWEEPS + 1):
+        strip_rows(s0, k, k, BAND - k, coef0)
+        rim(0, k)
     even = (2 * lane) % 128
 
     def coarsen(b, new):
@@ -346,7 +412,13 @@
                 )
             xs[4 * b + q] = jnp.where(low_half, pair[0], pair[1])
 
-    sweeps(0, coarsen)
+    for b in range(ROWS // 8):
+        new = []
+        for r in range(8 * b, 8 * b + 8):
+            m, base = (r + ASWEEPS, 0) if r < 16 else (r - 16 + ASWEEPS, 64)
+            new.append(merged(0, r, s0[ASWEEPS, m], base))
+            store_rows(0, r, new[-1])
+        coarsen(b, new)
 
     def block_transpose(x):
         for bit in (8, 4, 2, 1):
@@ -381,15 +453,46 @@
 
     for n in (SIDE_RIGHT, SIDE_LEFT, GR_TOP, GR_BOT, *range(SIDE_DIAG, SIDE_DIAG + 4)):
         sends[n].wait_recv()
-    kvs[0] = group_kappa(1)
-    kvs[1] = group_kappa(2)
-
-    def each(g, carry):
-        unpack(g, lambda h, g=g: rr[HALF_AT[h] + g - 1], lambda h, g=g: rl[HALF_AT[h] + g - 1])
-        sweeps(g, lambda b, new: None)
-        return carry
-
-    lax.fori_loop(1, 3, each, 0)
+    clear_outside(1)
+    clear_outside(2)
+    strips = [
+        [rl[at] for at in HALF_AT],
+        [pltpu.roll(rl[at + 1], 64, 1) for at in HALF_AT],
+        [pltpu.roll(rr[at], 56, 1) for at in HALF_AT],
+        [pltpu.roll(rr[at + 1], 120, 1) for at in HALF_AT],
+    ]
+    for i in range(EXT):
+        h, q = (i + 10) // 16, (i + 10) % 16
+        z = strip_halo(*(x[h] for x in strips), q)
+        if ASWEEPS <= i < EXT - ASWEEPS:
+            own = own12[i]
+        else:
+            own = jnp.where(
+                low_half,
+                own_strip(tt[0, 1, i, 0], tt[0, 1, i, 1], 0),
+                own_strip(tt[0, 2, i, 0], tt[0, 2, i, 1], 64),
+            )
+        z = jnp.where(strip_edge, z, own)
+        if i < ASWEEPS:
+            z = z * top_flag
+        if i >= EXT - ASWEEPS:
+            z = z * bot_flag
+        s12[0, i] = z
+
+    def coef12(i):
+        if i < ASWEEPS:
+            return keep12 * top_flag, kap12 * top_flag
+        if i >= EXT - ASWEEPS:
+            return keep12 * bot_flag, kap12 * bot_flag
+        return keep12, kap12
+
+    for k in range(1, ASWEEPS + 1):
+        strip_rows(s12, k, k, EXT - k, coef12)
+        rim(1, k)
+        rim(2, k)
+    for r in range(ROWS):
+        for g in (1, 2):
+            store_rows(g, r, merged(g, r, s12[ASWEEPS, ASWEEPS + r], 64 * (g - 1)))
 
     for n in (OC_TOP, OC_BOT):
         sends[n].wait_recv()
@@ -546,9 +649,11 @@
             vm((ROWS, COLS), f32),
             vm((OROWS, OCOLS), jnp.int32),
             vm((GX, 128), jnp.int32),
-            vm((3, EXT, 3) + v, f32),
-            vm((3, EXT, 3) + v, f32),
-            vm((3, EXT, 3) + v, f32),
+            vm((ASWEEPS + 1, 3, EXT, 2) + v, f32),
+            vm((ASWEEPS + 1, BAND) + v, f32),
+            vm((ASWEEPS + 1, EXT) + v, f32),
+            vm((BAND,) + v, f32),
+            vm((EXT,) + v, f32),
             vm((2,) + v, f32), vm((2,) + v, f32), vm((4,) + v, f32), vm((4,) + v, f32),
             vm((24,) + v, f32), vm((24,) + v, f32), vm((38,) + v, f32), vm((38,) + v, f32),
             vm((8,) + v, f32), vm((8,) + v, f32), vm((8,) + v, f32), vm((8,) + v, f32),
@@ -558,7 +663,6 @@
             vm((2, 48, 128), f32),
             vm((2, 5, 32, 128), f32),
             vm((OROWS, OCOLS), f32),
-            vm((2,) + v, f32),
             vm((16,) + v, f32), vm((16,) + v, f32), vm((16,) + v, f32),
             pltpu.SemaphoreType.DMA((18,)),
             pltpu.SemaphoreType.DMA((N_HALO,)),

time: 22.6 us -> 21.7 us (0.960)
  Pallas kernels: 21.9 us -> 20.9 us
    pallas_call x1, Pallas kernels: 20.8 us -> 19.9 us  [per_device(): pl.pallas_call(body, out_shape=tuple((pltpu.VMEM(shape, f32) for shape in...]
where the time goes in v4:
time: 21.7 us; the launch traced here: 21.6 us
  Pallas kernels  20.9 us (96%)
  between operations  0.64 us (3%)
    pallas_call x1, Pallas kernels, per_device(): pl.pallas_call(body, out_shape=tuple((pltpu.VMEM(shape, f32) for shape in...  19.9 us
    pallas_call x1, Pallas kernels, per_device(): pl.pallas_call(write_out, out_shape=tuple((pltpu.HBM(shape, f32) for shap...  1.03 us

profile of v4, /device:TPU:1, one launch (start us, length us, event | category | flops | bytes accessed | tf_op | source)
XLA Modules:
  0.0 21.6 jit_solution(6217584879028873557)
XLA Ops:
  0.6 19.9 %shard_map.112 = (f32[2,24,32,128]{3,2,1,0:T(8,128)S(1)}, f32[8,16,128]{2,1,0:T(8,128)S(1)}, f32[2,8,16,128]{3,2,1,0:T(8,128)S(1)}) custom-call(f32[4,6]{1,0:T(4,128)} %bitcast.4, f32[2,8]{1,0:T(2,128)} %okappa_in.1, f32[2,6]{1,0:T(2,128)} %gain_in.1, s32[1,16]{1,0:T(1,128)} %bitcast.5, f32[6,4,32,256]{3,2,1,0:T(8,128)} %atm.1, f32[32,256]{1,0:T(8,128)} %iw_in.1, ...), custom_call_target="tpu_custom_call" | custom-call | tf_op jit(solution)/shard_map/pallas_call | solution.py:640
  20.5 1.0 %shard_map.113 = (f32[6,4,32,256]{3,2,1,0:T(8,128)}, f32[6,16,128]{2,1,0:T(8,128)}, f32[2,8,16,128]{3,2,1,0:T(8,128)}) custom-call(f32[2,24,32,128]{3,2,1,0:T(8,128)S(1)} %get-tuple-element.6.outst, f32[8,16,128]{2,1,0:T(8,128)S(1)} %get-tuple-element.7.fout, f32[2,8,16,128]{3,2,1,0:T(8,128)S(1)} %get-tuple-element.8.oout), custom_call_target="tpu_custom_call" | custom-call | tf_op jit(solution)/shard_map/pallas_call | solution.py:687

commit v5 on v4

--- a/solution.py
+++ b/solution.py
@@ -14,7 +14,7 @@
 OROWS, OCOLS = 16, 128
 EXT = ROWS + 2 * ASWEEPS
 OEXT = OROWS + 2 * OSWEEPS
-BAND = 16 + 2 * ASWEEPS
+BAND = 8 + 2 * ASWEEPS
 MESH = pl.DeviceIdType.MESH
 
 ORDER = (
@@ -38,7 +38,7 @@
     outst, fout, oout,
     kappa, okappa, gain, rcnt,
     stage, ostage, iw, maskv, rmap,
-    tt, s0, s12, own0, own12,
+    tt, s0l, s0r, s12, own0, own12,
     gsl, gsr, grr, grl,
     sl, sr, rr, rl,
     su, sd, ru, rd,
@@ -125,13 +125,8 @@
 
     def put_own(g, r, x0, x1):
         if g == 0:
-            if r < 16 + ASWEEPS:
-                own0[r + ASWEEPS] = own_strip(x0, x1, 0)
-            if r >= 16 - ASWEEPS:
-                m = r - 16 + ASWEEPS
-                y = own_strip(x0, x1, 64)
-                own0[m] = y if m < ASWEEPS else jnp.where(low_half, own0[m], y)
-        elif g == 1:
+            return
+        if g == 1:
             own12[r + ASWEEPS] = own_strip(x0, x1, 0)
         else:
             own12[r + ASWEEPS] = jnp.where(
@@ -184,6 +179,19 @@
         gsr[half] = x
 
     transpose_group(0, put_gsl, put_gsr)
+    quarter = lane // 32
+
+    def own_band(side, m, bands, y=None):
+        for b in bands:
+            z = pltpu.roll(tt[0, 0, 8 * b + m, side], 32 * b + (24 if side else 8), 1)
+            y = z if y is None else jnp.where(quarter == b, z, y)
+        return y
+
+    for side in range(2):
+        for m in range(BAND):
+            bands = [b for b in range(4) if 0 <= 8 * b + m - ASWEEPS < ROWS]
+            own0[side, m] = own_band(side, m, bands)
+
     top_rows = pl.ds(0, ASWEEPS)
     own_first = pl.ds(ASWEEPS, ASWEEPS)
     own_last = pl.ds(ROWS, ASWEEPS)
@@ -224,6 +232,29 @@
         sl[4 + j] = jnp.where(c_lo, x[0], pltpu.roll(x[1], 4, 1))
         sr[4 + j] = jnp.where(c_lo, pltpu.roll(x[1], 124, 1), x[0])
 
+    pl.semaphore_wait(barrier, 8 + GX - 3)
+
+    send(gsl.at[pl.ds(1, 1)], grr.at[pl.ds(0, 1)], G0_DIAG, left, down)
+    send(gsl.at[pl.ds(0, 1)], grr.at[pl.ds(3, 1)], G0_DIAG + 1, left, up)
+    send(gsr.at[pl.ds(1, 1)], grl.at[pl.ds(0, 1)], G0_DIAG + 2, right, down)
+    send(gsr.at[pl.ds(0, 1)], grl.at[pl.ds(3, 1)], G0_DIAG + 3, right, up)
+    send(gsl, grr.at[pl.ds(1, 2)], G0_RIGHT, left, gy)
+    send(gsr, grl.at[pl.ds(1, 2)], G0_LEFT, right, gy)
+    send(tt.at[0, 0, own_last], tt.at[0, 0, top_rows], G0_TOP, gx, down)
+    send(tt.at[0, 0, own_first], tt.at[0, 0, bot_rows], G0_BOT, gx, up)
+
+    rest = pl.ds(1, 2)
+    send(sl, rr.at[pl.ds(7, 24)], SIDE_RIGHT, left, gy)
+    send(sr, rl.at[pl.ds(7, 24)], SIDE_LEFT, right, gy)
+    send(tt.at[0, rest, own_last], tt.at[0, rest, top_rows], GR_TOP, gx, down)
+    send(tt.at[0, rest, own_first], tt.at[0, rest, bot_rows], GR_BOT, gx, up)
+    send(sl.at[pl.ds(17, 7)], rr.at[pl.ds(0, 7)], SIDE_DIAG, left, down)
+    send(sl.at[pl.ds(0, 7)], rr.at[pl.ds(31, 7)], SIDE_DIAG + 1, left, up)
+    send(sr.at[pl.ds(17, 7)], rl.at[pl.ds(0, 7)], SIDE_DIAG + 2, right, down)
+    send(sr.at[pl.ds(0, 7)], rl.at[pl.ds(31, 7)], SIDE_DIAG + 3, right, up)
+    send(sd, ru, OC_TOP, gx, down)
+    send(su, rd, OC_BOT, gx, up)
+
     top_flag = jnp.where(gy == 0, 0.0, 1.0).astype(jnp.float32)
     bot_flag = jnp.where(gy == GY - 1, 0.0, 1.0).astype(jnp.float32)
     for c in scalars:
@@ -282,10 +313,10 @@
 
     strip_edge = (slot16 % 8 == 0) | (slot16 % 8 == 7)
 
-    def strip_halo(a, b, c, d, q):
-        z = jnp.where(slot16 == (q + 7) % 16, c, d)
-        z = jnp.where(slot16 == (q + 8) % 16, b, z)
-        z = jnp.where(slot16 == q, a, z)
+    def strip_halo(parts, q):
+        z = None
+        for at, x in parts:
+            z = x if z is None else jnp.where(slot16 == (q + at) % 16, x, z)
         return z if q == 0 else pltpu.roll(z, 128 - 8 * q, 1)
 
     def strip_rows(ref, k, lo, hi, coef):
@@ -297,15 +328,13 @@
                 (u + d) + (pltpu.roll(c, 1, 1) + pltpu.roll(c, 127, 1))
             )
 
-    def merged(g, r, strip, base):
-        x0, x1 = tt[ASWEEPS, g, ASWEEPS + r, 0], tt[ASWEEPS, g, ASWEEPS + r, 1]
-        y0 = pltpu.roll(strip, 120 - base, 1)
-        y1 = pltpu.roll(strip, (72 - base) % 128, 1)
-        return [jnp.where(lane < 8, y0, x0), jnp.where(lane >= 120, y1, x1)]
-
-    def store_rows(g, r, new):
-        for t in range(2):
-            outst2[t, pl.ds(g * 8 * ROWS + r, 8, stride=ROWS), :] = new[t]
+    def merged_side(g, r, side, strip, shift):
+        x = tt[ASWEEPS, g, ASWEEPS + r, side]
+        here = lane >= 120 if side else lane < 8
+        return jnp.where(here, pltpu.roll(strip, shift % 128, 1), x)
+
+    def store_row(g, r, t, new):
+        outst2[t, pl.ds(g * 8 * ROWS + r, 8, stride=ROWS), :] = new
 
     rcopy.wait()
     hot_c, hot_j = [], []
@@ -328,97 +357,75 @@
     live[...] = lax.dot_general(fold, own, contract, preferred_element_type=jnp.float32)
 
     interior(0)
-    pl.semaphore_wait(barrier, 8 + GX - 3)
-
-    send(gsl.at[pl.ds(1, 1)], grr.at[pl.ds(0, 1)], G0_DIAG, left, down)
-    send(gsl.at[pl.ds(0, 1)], grr.at[pl.ds(3, 1)], G0_DIAG + 1, left, up)
-    send(gsr.at[pl.ds(1, 1)], grl.at[pl.ds(0, 1)], G0_DIAG + 2, right, down)
-    send(gsr.at[pl.ds(0, 1)], grl.at[pl.ds(3, 1)], G0_DIAG + 3, right, up)
-    send(gsl, grr.at[pl.ds(1, 2)], G0_RIGHT, left, gy)
-    send(gsr, grl.at[pl.ds(1, 2)], G0_LEFT, right, gy)
-    send(tt.at[0, 0, own_last], tt.at[0, 0, top_rows], G0_TOP, gx, down)
-    send(tt.at[0, 0, own_first], tt.at[0, 0, bot_rows], G0_BOT, gx, up)
-
-    rest = pl.ds(1, 2)
-    send(sl, rr.at[pl.ds(7, 24)], SIDE_RIGHT, left, gy)
-    send(sr, rl.at[pl.ds(7, 24)], SIDE_LEFT, right, gy)
-    send(tt.at[0, rest, own_last], tt.at[0, rest, top_rows], GR_TOP, gx, down)
-    send(tt.at[0, rest, own_first], tt.at[0, rest, bot_rows], GR_BOT, gx, up)
-    send(sl.at[pl.ds(17, 7)], rr.at[pl.ds(0, 7)], SIDE_DIAG, left, down)
-    send(sl.at[pl.ds(0, 7)], rr.at[pl.ds(31, 7)], SIDE_DIAG + 1, left, up)
-    send(sr.at[pl.ds(17, 7)], rl.at[pl.ds(0, 7)], SIDE_DIAG + 2, right, down)
-    send(sr.at[pl.ds(0, 7)], rl.at[pl.ds(31, 7)], SIDE_DIAG + 3, right, up)
-    send(sd, ru, OC_TOP, gx, down)
-    send(su, rd, OC_BOT, gx, up)
-
     interior(1)
     interior(2)
 
-    for n in range(8):
+    band_top = jnp.where(quarter == 0, top_flag, 1.0)
+    band_bot = jnp.where(quarter == 3, bot_flag, 1.0)
+
+    def band_flag(m):
+        if m < ASWEEPS:
+            return band_top
+        return band_bot if m >= BAND - ASWEEPS else None
+
+    def band_coef(m):
+        flag = band_flag(m)
+        if flag is None:
+            return keeps[0], kaps[0]
+        return keeps[0] * flag, kaps[0] * flag
+
+    def band_strips(ref, side, got_strips):
+        at = [4 * b + (3 if side else 0) for b in range(4)]
+        turn = [8 * (at[b] - 8 * (b % 2)) % 128 for b in range(4)]
+        strips = [
+            [x if n == 0 else pltpu.roll(x, n, 1) for x in (got_strips[h] for h in range(4))]
+            for n in turn
+        ]
+        edge = slot16 % 4 == (3 if side else 0)
+        for m in range(BAND):
+            q = (m + 10) % 16
+            z = strip_halo([(at[b], strips[b][(8 * b + m + 10) // 16]) for b in range(4)], q)
+            own = own0[side, m]
+            if m < ASWEEPS:
+                own = jnp.where(quarter == 0, own_band(side, m, (0,)), own)
+            if m >= BAND - ASWEEPS:
+                own = jnp.where(quarter == 3, own_band(side, m, (3,)), own)
+            z = jnp.where(edge, z, own)
+            flag = band_flag(m)
+            ref[0, m] = z if flag is None else z * flag
+
+    even = (2 * lane) % 128
+
+    def pair_sum(b, q, t, new):
+        total = None
+        for e in range(2):
+            at = 2 * q + e
+            w = iw[pl.ds(8 * b + at, 1), 128 * t : 128 * t + 128]
+            term = new[at] * w
+            total = term if total is None else total + term
+        total = total + pltpu.roll(total, 127, 1)
+        return jnp.take_along_axis(total, even, axis=1, mode="promise_in_bounds")
+
+    for n in (G0_TOP, G0_BOT, G0_LEFT, G0_DIAG + 2, G0_DIAG + 3):
         sends[n].wait_recv()
     wcopy.wait()
     clear_outside(0)
-    low_top = jnp.where(low_half, top_flag, 1.0)
-    high_bot = jnp.where(low_half, 1.0, bot_flag)
-    strips = [
-        [grl[h] for h in range(4)],
-        [pltpu.roll(grl[h], 64, 1) for h in range(4)],
-        [pltpu.roll(grr[h], 56, 1) for h in range(4)],
-        [pltpu.roll(grr[h], 120, 1) for h in range(4)],
-    ]
-    for m in range(BAND):
-        h, q = (m + 10) // 16, (m + 10) % 16
-        z = strip_halo(strips[0][h], strips[1][h + 1], strips[2][h], strips[3][h + 1], q)
-        own = own0[m]
-        if m < ASWEEPS:
-            own = jnp.where(low_half, own_strip(tt[0, 0, m, 0], tt[0, 0, m, 1], 0), own)
-        if m >= BAND - ASWEEPS:
-            own = jnp.where(
-                low_half, own, own_strip(tt[0, 0, m + 16, 0], tt[0, 0, m + 16, 1], 64)
+    band_strips(s0l, 0, grl)
+    for k in range(1, ASWEEPS + 1):
+        strip_rows(s0l, k, k, BAND - k, band_coef)
+        rim(0, k)
+    for b in range(4):
+        new = [[], []]
+        for e in range(8):
+            r = 8 * b + e
+            x = merged_side(0, r, 0, s0l[ASWEEPS, ASWEEPS + e], 120 - 32 * b)
+            store_row(0, r, 0, x)
+            new[0].append(x)
+            new[1].append(tt[ASWEEPS, 0, ASWEEPS + r, 1])
+        for q in range(4):
+            xs[4 * b + q] = jnp.where(
+                low_half, pair_sum(b, q, 0, new[0]), pair_sum(b, q, 1, new[1])
             )
-        z = jnp.where(strip_edge, z, own)
-        if m < ASWEEPS:
-            z = z * low_top
-        if m >= BAND - ASWEEPS:
-            z = z * high_bot
-        s0[0, m] = z
-
-    def coef0(m):
-        if m < ASWEEPS:
-            return keeps[0] * low_top, kaps[0] * low_top
-        if m >= BAND - ASWEEPS:
-            return keeps[0] * high_bot, kaps[0] * high_bot
-        return keeps[0], kaps[0]
-
-    for k in range(1, ASWEEPS + 1):
-        strip_rows(s0, k, k, BAND - k, coef0)
-        rim(0, k)
-    even = (2 * lane) % 128
-
-    def coarsen(b, new):
-        weights = iw[pl.ds(8 * b, 8), :]
-        for q in range(4):
-            pair = []
-            for t in range(2):
-                total = None
-                for e in range(2):
-                    at = 2 * q + e
-                    w = weights[at : at + 1, 128 * t : 128 * t + 128]
-                    term = new[2 * q + e][t] * w
-                    total = term if total is None else total + term
-                total = total + pltpu.roll(total, 127, 1)
-                pair.append(
-                    jnp.take_along_axis(total, even, axis=1, mode="promise_in_bounds")
-                )
-            xs[4 * b + q] = jnp.where(low_half, pair[0], pair[1])
-
-    for b in range(ROWS // 8):
-        new = []
-        for r in range(8 * b, 8 * b + 8):
-            m, base = (r + ASWEEPS, 0) if r < 16 else (r - 16 + ASWEEPS, 64)
-            new.append(merged(0, r, s0[ASWEEPS, m], base))
-            store_rows(0, r, new[-1])
-        coarsen(b, new)
 
     def block_transpose(x):
         for bit in (8, 4, 2, 1):
@@ -432,11 +439,11 @@
             x = y
         return x
 
-    for d, x in enumerate(block_transpose([xs[j] for j in range(16)])):
+    for d, x in enumerate(block_transpose([xs[j] for j in range(16)])[:15]):
         msg[d] = x
 
     def remap(k):
-        to = lax.rem(gx + k, GX)
+        to = k - 1 + jnp.where(k > gx, 1, 0)
         return pltpu.make_async_remote_copy(
             src_ref=msg.at[to],
             dst_ref=got.at[gx],
@@ -447,8 +454,29 @@
         )
 
     moves = [remap(k) for k in range(1, GX)]
-    for c in moves:
+    for c in moves[:-1]:
         c.start()
+
+    for n in (G0_RIGHT, G0_DIAG, G0_DIAG + 1):
+        sends[n].wait_recv()
+    band_strips(s0r, 1, grr)
+    for k in range(1, ASWEEPS + 1):
+        strip_rows(s0r, k, k, BAND - k, band_coef)
+    last_block = None
+    for b in range(4):
+        new = []
+        for e in range(8):
+            r = 8 * b + e
+            x = merged_side(0, r, 1, s0r[ASWEEPS, ASWEEPS + e], 104 - 32 * b)
+            store_row(0, r, 1, x)
+            new.append(x)
+        for q in range(4):
+            j = 4 * b + q
+            x = pair_sum(b, q, 1, new)
+            x = x if j == 15 else pltpu.roll(x, 8 * j + 8, 1)
+            last_block = x if last_block is None else jnp.where(slot16 == j, x, last_block)
+    msg[15] = last_block
+    moves[-1].start()
     got[gx] = msg[gx]
 
     for n in (SIDE_RIGHT, SIDE_LEFT, GR_TOP, GR_BOT, *range(SIDE_DIAG, SIDE_DIAG + 4)):
@@ -463,7 +491,7 @@
     ]
     for i in range(EXT):
         h, q = (i + 10) // 16, (i + 10) % 16
-        z = strip_halo(*(x[h] for x in strips), q)
+        z = strip_halo(list(zip((0, 8, 7, 15), (x[h] for x in strips))), q)
         if ASWEEPS <= i < EXT - ASWEEPS:
             own = own12[i]
         else:
@@ -492,7 +520,10 @@
         rim(2, k)
     for r in range(ROWS):
         for g in (1, 2):
-            store_rows(g, r, merged(g, r, s12[ASWEEPS, ASWEEPS + r], 64 * (g - 1)))
+            base = 64 * (g - 1)
+            for t, shift in ((0, 120 - base), (1, 72 - base)):
+                x = merged_side(g, r, t, s12[ASWEEPS, ASWEEPS + r], shift)
+                store_row(g, r, t, x)
 
     for n in (OC_TOP, OC_BOT):
         sends[n].wait_recv()
@@ -500,8 +531,8 @@
         for t in range(2):
             c0[i, t] = ru[2 * i + t]
             c0[OSWEEPS + OROWS + i, t] = rd[2 + 2 * i + t]
-    wrap_right = jnp.where(gx == GX - 1, 120, 0)
-    wrap_left = jnp.where(gx == 0, 8, 0)
+    wrap_right = jnp.where(gx == GX - 1, 0, 8)
+    wrap_left = jnp.where(gx == 0, 0, 120)
     for i in range(OEXT):
         at = i if i < 3 else (i + 8 if i < 19 else i + 16)
         x = pltpu.roll(rr[at], wrap_right, 1)
@@ -525,8 +556,8 @@
         n = [mnat[e, r0 - 1 : r0 + 7, :] for e in range(2)]
         s = [mnat[e, r0 + 1 : r0 + 9, :] for e in range(2)]
         for e in range(2):
-            ke = m[e] * jnp.where(in8 == 7, pltpu.roll(m[1 - e], 7, 1), pltpu.roll(m[e], 127, 1))
-            kw = m[e] * jnp.where(in8 == 0, pltpu.roll(m[1 - e], 121, 1), pltpu.roll(m[e], 1, 1))
+            ke = m[e] * pltpu.roll(jnp.where(in8 == 0, m[1 - e], m[e]), 127, 1)
+            kw = m[e] * pltpu.roll(jnp.where(in8 == 7, m[1 - e], m[e]), 1, 1)
             kn = m[e] * n[e]
             ks = m[e] * s[e]
             for which, value in enumerate((ke, kw, kn, ks, (ke + kw) + (kn + ks))):
@@ -549,8 +580,8 @@
                 for t in range(2):
                     me, other = src[e], src[1 - e]
                     o, x = me[i, t], other[i, t]
-                    east = jnp.where(in8 == 7, pltpu.roll(x, 7, 1), pltpu.roll(o, 127, 1))
-                    west = jnp.where(in8 == 0, pltpu.roll(x, 121, 1), pltpu.roll(o, 1, 1))
+                    east = pltpu.roll(jnp.where(in8 == 0, x, o), 127, 1)
+                    west = pltpu.roll(jnp.where(in8 == 7, x, o), 1, 1)
                     flux = (co[0] * east + co[1] * west) + (
                         co[2] * me[i - 1, t] + co[3] * me[i + 1, t]
                     )
@@ -651,8 +682,9 @@
             vm((GX, 128), jnp.int32),
             vm((ASWEEPS + 1, 3, EXT, 2) + v, f32),
             vm((ASWEEPS + 1, BAND) + v, f32),
+            vm((ASWEEPS + 1, BAND) + v, f32),
             vm((ASWEEPS + 1, EXT) + v, f32),
-            vm((BAND,) + v, f32),
+            vm((2, BAND) + v, f32),
             vm((EXT,) + v, f32),
             vm((2,) + v, f32), vm((2,) + v, f32), vm((4,) + v, f32), vm((4,) + v, f32),
             vm((24,) + v, f32), vm((24,) + v, f32), vm((38,) + v, f32), vm((38,) + v, f32),

time: 21.7 us -> 20 us (0.922)
  Pallas kernels: 20.9 us -> 19.2 us
    pallas_call x1, Pallas kernels: 19.9 us -> 18.1 us  [per_device(): pl.pallas_call(body, out_shape=tuple((pltpu.VMEM(shape, f32) for shape in...]
where the time goes in v5:
time: 20 us; the launch traced here: 19.8 us
  Pallas kernels  19.2 us (96%)
  between operations  0.64 us (3%)
    pallas_call x1, Pallas kernels, per_device(): pl.pallas_call(body, out_shape=tuple((pltpu.VMEM(shape, f32) for shape in...  18.1 us
    pallas_call x1, Pallas kernels, per_device(): pl.pallas_call(write_out, out_shape=tuple((pltpu.HBM(shape, f32) for shap...  1.03 us

profile of v5, /device:TPU:1, one launch (start us, length us, event | category | flops | bytes accessed | tf_op | source)
XLA Modules:
  0.0 19.8 jit_solution(5835695135479742971)
XLA Ops:
  0.6 18.1 %shard_map.112 = (f32[2,24,32,128]{3,2,1,0:T(8,128)S(1)}, f32[8,16,128]{2,1,0:T(8,128)S(1)}, f32[2,8,16,128]{3,2,1,0:T(8,128)S(1)}) custom-call(f32[4,6]{1,0:T(4,128)} %bitcast.4, f32[2,8]{1,0:T(2,128)} %okappa_in.1, f32[2,6]{1,0:T(2,128)} %gain_in.1, s32[1,16]{1,0:T(1,128)} %bitcast.5, f32[6,4,32,256]{3,2,1,0:T(8,128)} %atm.1, f32[32,256]{1,0:T(8,128)} %iw_in.1, ...), custom_call_target="tpu_custom_call" | custom-call | tf_op jit(solution)/shard_map/pallas_call | solution.py:671
  18.8 1.0 %shard_map.113 = (f32[6,4,32,256]{3,2,1,0:T(8,128)}, f32[6,16,128]{2,1,0:T(8,128)}, f32[2,8,16,128]{3,2,1,0:T(8,128)}) custom-call(f32[2,24,32,128]{3,2,1,0:T(8,128)S(1)} %get-tuple-element.6.outst, f32[8,16,128]{2,1,0:T(8,128)S(1)} %get-tuple-element.7.fout, f32[2,8,16,128]{3,2,1,0:T(8,128)S(1)} %get-tuple-element.8.oout), custom_call_target="tpu_custom_call" | custom-call | tf_op jit(solution)/shard_map/pallas_call | solution.py:719

commit v6 on v5

--- a/solution.py
+++ b/solution.py
@@ -29,6 +29,7 @@
 GR_TOP, GR_BOT, SIDE_RIGHT, SIDE_LEFT, SIDE_DIAG = 8, 9, 10, 11, 12
 OC_TOP, OC_BOT = 16, 17
 N_HALO = 18
+BATCH = (0, 0, 1, 0, 1, 1, 0, 0) + (2,) * 8 + (3, 3)
 HALF_AT = (5, 7, 29, 31)
 
 
@@ -154,19 +155,21 @@
             put_left(half, pack_l)
             put_right(half, pack_r)
 
-    sends = {}
 
     def send(src, dst, sem, a, b):
         c = pltpu.make_async_remote_copy(
             src_ref=src,
             dst_ref=dst,
-            send_sem=hs_sem.at[sem],
-            recv_sem=hr_sem.at[sem],
+            send_sem=hs_sem,
+            recv_sem=hr_sem.at[BATCH[sem]],
             device_id={"gx": a, "gy": b},
             device_id_type=MESH,
         )
         c.start()
-        sends[sem] = c
+
+    def halo_wait(batch, pairs):
+        ref = tt.at[0, pl.ds(0, 2), pl.ds(0, pairs // 2)]
+        pltpu.make_async_copy(ref, ref, hr_sem.at[batch]).wait()
 
     for n in (0, 1):
         for c in ins[n]:
@@ -406,8 +409,7 @@
         total = total + pltpu.roll(total, 127, 1)
         return jnp.take_along_axis(total, even, axis=1, mode="promise_in_bounds")
 
-    for n in (G0_TOP, G0_BOT, G0_LEFT, G0_DIAG + 2, G0_DIAG + 3):
-        sends[n].wait_recv()
+    halo_wait(0, 14)
     wcopy.wait()
     clear_outside(0)
     band_strips(s0l, 0, grl)
@@ -447,8 +449,8 @@
         return pltpu.make_async_remote_copy(
             src_ref=msg.at[to],
             dst_ref=got.at[gx],
-            send_sem=as_sem.at[k],
-            recv_sem=ar_sem.at[gx],
+            send_sem=as_sem,
+            recv_sem=ar_sem,
             device_id={"gx": to, "gy": gy},
             device_id_type=MESH,
         )
@@ -457,8 +459,7 @@
     for c in moves[:-1]:
         c.start()
 
-    for n in (G0_RIGHT, G0_DIAG, G0_DIAG + 1):
-        sends[n].wait_recv()
+    halo_wait(1, 2)
     band_strips(s0r, 1, grr)
     for k in range(1, ASWEEPS + 1):
         strip_rows(s0r, k, k, BAND - k, band_coef)
@@ -479,8 +480,7 @@
     moves[-1].start()
     got[gx] = msg[gx]
 
-    for n in (SIDE_RIGHT, SIDE_LEFT, GR_TOP, GR_BOT, *range(SIDE_DIAG, SIDE_DIAG + 4)):
-        sends[n].wait_recv()
+    halo_wait(2, 62)
     clear_outside(1)
     clear_outside(2)
     strips = [
@@ -525,8 +525,7 @@
                 x = merged_side(g, r, t, s12[ASWEEPS, ASWEEPS + r], shift)
                 store_row(g, r, t, x)
 
-    for n in (OC_TOP, OC_BOT):
-        sends[n].wait_recv()
+    halo_wait(3, 8)
     for i in range(OSWEEPS):
         for t in range(2):
             c0[i, t] = ru[2 * i + t]
@@ -594,16 +593,8 @@
         for i in range(k, OEXT - k):
             step(i)
 
-    for k in range(1, GX):
-        frm = lax.rem(gx + k, GX)
-        pltpu.make_async_remote_copy(
-            src_ref=msg.at[frm],
-            dst_ref=got.at[frm],
-            send_sem=as_sem.at[k],
-            recv_sem=ar_sem.at[frm],
-            device_id={"gx": frm, "gy": gy},
-            device_id_type=MESH,
-        ).wait_recv()
+    arrived = pl.ds(0, GX - 1)
+    pltpu.make_async_copy(msg.at[arrived], got.at[arrived], ar_sem).wait()
     for j, x in enumerate(block_transpose([got[s] for s in range(16)])):
         fout2[pl.ds(j, 8, stride=OROWS), :] = x * live[j : j + 1, :]
     wet = maskv[...].astype(jnp.float32)
@@ -613,10 +604,9 @@
             term = gain[t, f] * fout[f]
             pushed = term if pushed is None else pushed + term
         oout[t, 0] = oout[t, 0] + wet * pushed
-    for c in sends.values():
-        c.wait_send()
-    for c in moves:
-        c.wait_send()
+    sent = tt.at[0, pl.ds(0, 2), pl.ds(0, 43)]
+    pltpu.make_async_copy(sent, sent, hs_sem).wait()
+    pltpu.make_async_copy(msg.at[arrived], got.at[arrived], as_sem).wait()
 
 
 def write_out(outst, fout, oout, atm_out, forc_out, oce_out, sem):
@@ -697,10 +687,10 @@
             vm((OROWS, OCOLS), f32),
             vm((16,) + v, f32), vm((16,) + v, f32), vm((16,) + v, f32),
             pltpu.SemaphoreType.DMA((18,)),
-            pltpu.SemaphoreType.DMA((N_HALO,)),
-            pltpu.SemaphoreType.DMA((N_HALO,)),
-            pltpu.SemaphoreType.DMA((GX,)),
-            pltpu.SemaphoreType.DMA((GX,)),
+            pltpu.SemaphoreType.DMA,
+            pltpu.SemaphoreType.DMA((4,)),
+            pltpu.SemaphoreType.DMA,
+            pltpu.SemaphoreType.DMA,
         ],
         compiler_params=pltpu.CompilerParams(
             collective_id=0, has_side_effects=True, vmem_limit_bytes=32 * 1024 * 1024

time: 20 us -> 19.3 us (0.965)
  Pallas kernels: 19.2 us -> 18.5 us
    pallas_call x1, Pallas kernels: 18.1 us -> 17.5 us  [per_device(): pl.pallas_call(body, out_shape=tuple((pltpu.VMEM(shape, f32) for shape in...]
where the time goes in v6:
time: 19.3 us; the launch traced here: 19.2 us
  Pallas kernels  18.5 us (96%)
  between operations  0.64 us (3%)
    pallas_call x1, Pallas kernels, per_device(): pl.pallas_call(body, out_shape=tuple((pltpu.VMEM(shape, f32) for shape in...  17.5 us
    pallas_call x1, Pallas kernels, per_device(): pl.pallas_call(write_out, out_shape=tuple((pltpu.HBM(shape, f32) for shap...  1.03 us

profile of v6, /device:TPU:1, one launch (start us, length us, event | category | flops | bytes accessed | tf_op | source)
XLA Modules:
  0.0 19.2 jit_solution(759213874323406948)
XLA Ops:
  0.6 17.5 %shard_map.112 = (f32[2,24,32,128]{3,2,1,0:T(8,128)S(1)}, f32[8,16,128]{2,1,0:T(8,128)S(1)}, f32[2,8,16,128]{3,2,1,0:T(8,128)S(1)}) custom-call(f32[4,6]{1,0:T(4,128)} %bitcast.4, f32[2,8]{1,0:T(2,128)} %okappa_in.1, f32[2,6]{1,0:T(2,128)} %gain_in.1, s32[1,16]{1,0:T(1,128)} %bitcast.5, f32[6,4,32,256]{3,2,1,0:T(8,128)} %atm.1, f32[32,256]{1,0:T(8,128)} %iw_in.1, ...), custom_call_target="tpu_custom_call" | custom-call | tf_op jit(solution)/shard_map/pallas_call | solution.py:661
  18.1 1.0 %shard_map.113 = (f32[6,4,32,256]{3,2,1,0:T(8,128)}, f32[6,16,128]{2,1,0:T(8,128)}, f32[2,8,16,128]{3,2,1,0:T(8,128)}) custom-call(f32[2,24,32,128]{3,2,1,0:T(8,128)S(1)} %get-tuple-element.6.outst, f32[8,16,128]{2,1,0:T(8,128)S(1)} %get-tuple-element.7.fout, f32[2,8,16,128]{3,2,1,0:T(8,128)S(1)} %get-tuple-element.8.oout), custom_call_target="tpu_custom_call" | custom-call | tf_op jit(solution)/shard_map/pallas_call | solution.py:709

commit v7 on v6

--- a/solution.py
+++ b/solution.py
@@ -59,7 +59,7 @@
             pltpu.make_async_copy(
                 atm.at[pl.ds(v, cnt), l, :, pl.ds(128 * t, 128)],
                 stage.at[t, pl.ds(p, cnt)],
-                in_sem.at[2 * n + t],
+                in_sem.at[0 if n < 2 else 1],
             )
             for t in range(2)
         ]
@@ -171,9 +171,8 @@
         ref = tt.at[0, pl.ds(0, 2), pl.ds(0, pairs // 2)]
         pltpu.make_async_copy(ref, ref, hr_sem.at[batch]).wait()
 
-    for n in (0, 1):
-        for c in ins[n]:
-            c.wait()
+    loaded = stage.at[:, pl.ds(0, 8)]
+    pltpu.make_async_copy(loaded, loaded, in_sem.at[0]).wait()
 
     def put_gsl(half, x):
         gsl[half] = x
@@ -200,9 +199,8 @@
     own_last = pl.ds(ROWS, ASWEEPS)
     bot_rows = pl.ds(ROWS + ASWEEPS, ASWEEPS)
 
-    for n in (2, 3, 4):
-        for c in ins[n]:
-            c.wait()
+    loaded = stage.at[:, pl.ds(8, 16)]
+    pltpu.make_async_copy(loaded, loaded, in_sem.at[1]).wait()
     for g in (1, 2):
 
         def put_sl(half, x, g=g):
@@ -247,14 +245,14 @@
     send(tt.at[0, 0, own_first], tt.at[0, 0, bot_rows], G0_BOT, gx, up)
 
     rest = pl.ds(1, 2)
-    send(sl, rr.at[pl.ds(7, 24)], SIDE_RIGHT, left, gy)
-    send(sr, rl.at[pl.ds(7, 24)], SIDE_LEFT, right, gy)
-    send(tt.at[0, rest, own_last], tt.at[0, rest, top_rows], GR_TOP, gx, down)
-    send(tt.at[0, rest, own_first], tt.at[0, rest, bot_rows], GR_BOT, gx, up)
     send(sl.at[pl.ds(17, 7)], rr.at[pl.ds(0, 7)], SIDE_DIAG, left, down)
     send(sl.at[pl.ds(0, 7)], rr.at[pl.ds(31, 7)], SIDE_DIAG + 1, left, up)
     send(sr.at[pl.ds(17, 7)], rl.at[pl.ds(0, 7)], SIDE_DIAG + 2, right, down)
     send(sr.at[pl.ds(0, 7)], rl.at[pl.ds(31, 7)], SIDE_DIAG + 3, right, up)
+    send(tt.at[0, rest, own_last], tt.at[0, rest, top_rows], GR_TOP, gx, down)
+    send(tt.at[0, rest, own_first], tt.at[0, rest, bot_rows], GR_BOT, gx, up)
+    send(sl, rr.at[pl.ds(7, 24)], SIDE_RIGHT, left, gy)
+    send(sr, rl.at[pl.ds(7, 24)], SIDE_LEFT, right, gy)
     send(sd, ru, OC_TOP, gx, down)
     send(su, rd, OC_BOT, gx, up)
 
@@ -562,6 +560,18 @@
             for which, value in enumerate((ke, kw, kn, ks, (ke + kw) + (kn + ks))):
                 ko[e, which, pl.ds(8 * b, 8), :] = value
 
+    arrived = pl.ds(0, GX - 1)
+    pltpu.make_async_copy(msg.at[arrived], got.at[arrived], ar_sem).wait()
+    for j, x in enumerate(block_transpose([got[s] for s in range(16)])):
+        fout2[pl.ds(j, 8, stride=OROWS), :] = x * live[j : j + 1, :]
+    pushes = []
+    for t in range(2):
+        pushed = None
+        for f in range(VARS):
+            term = gain[t, f] * fout[f]
+            pushed = term if pushed is None else pushed + term
+        pushes.append(maskv[...].astype(jnp.float32) * pushed)
+
     okap = []
     for t in range(2):
         k = jnp.zeros((8, 128), jnp.float32)
@@ -593,17 +603,8 @@
         for i in range(k, OEXT - k):
             step(i)
 
-    arrived = pl.ds(0, GX - 1)
-    pltpu.make_async_copy(msg.at[arrived], got.at[arrived], ar_sem).wait()
-    for j, x in enumerate(block_transpose([got[s] for s in range(16)])):
-        fout2[pl.ds(j, 8, stride=OROWS), :] = x * live[j : j + 1, :]
-    wet = maskv[...].astype(jnp.float32)
     for t in range(2):
-        pushed = None
-        for f in range(VARS):
-            term = gain[t, f] * fout[f]
-            pushed = term if pushed is None else pushed + term
-        oout[t, 0] = oout[t, 0] + wet * pushed
+        oout[t, 0] = oout[t, 0] + pushes[t]
     sent = tt.at[0, pl.ds(0, 2), pl.ds(0, 43)]
     pltpu.make_async_copy(sent, sent, hs_sem).wait()
     pltpu.make_async_copy(msg.at[arrived], got.at[arrived], as_sem).wait()
@@ -614,16 +615,17 @@
         pltpu.make_async_copy(
             outst.at[t, pl.ds(p, cnt)],
             atm_out.at[pl.ds(v, cnt), l, :, pl.ds(128 * t, 128)],
-            sem.at[2 * n + t],
+            sem.at[0],
         )
-        for n, (p, v, cnt, l) in enumerate(RUNS)
+        for p, v, cnt, l in RUNS
         for t in range(2)
     ]
-    copies.append(pltpu.make_async_copy(oout, oce_out, sem.at[10]))
-    copies.append(pltpu.make_async_copy(fout.at[pl.ds(0, VARS)], forc_out, sem.at[11]))
+    copies.append(pltpu.make_async_copy(oout, oce_out, sem.at[1]))
+    copies.append(pltpu.make_async_copy(fout.at[pl.ds(0, VARS)], forc_out, sem.at[2]))
     for c in copies:
         c.start()
-    for c in copies:
+    pltpu.make_async_copy(outst, outst, sem.at[0]).wait()
+    for c in copies[-2:]:
         c.wait()
 
 
@@ -711,7 +713,7 @@
         out_shape=tuple(pltpu.HBM(shape, f32) for shape in shapes),
         in_specs=[pl.BlockSpec(memory_space=pltpu.VMEM)] * 3,
         out_specs=(hbm, hbm, hbm),
-        scratch_shapes=[pltpu.SemaphoreType.DMA((12,))],
+        scratch_shapes=[pltpu.SemaphoreType.DMA((3,))],
         compiler_params=pltpu.CompilerParams(vmem_limit_bytes=4 * 1024 * 1024),
     )(*(pltpu.with_memory_space_constraint(x, pltpu.VMEM) for x in done))
 

time: 19.3 us -> 18.9 us (0.979)
  Pallas kernels: 18.5 us -> 18.1 us
    pallas_call x1, Pallas kernels: 17.5 us -> 17.1 us  [per_device(): pl.pallas_call(body, out_shape=tuple((pltpu.VMEM(shape, f32) for shape in...]
where the time goes in v7:
time: 18.9 us; the launch traced here: 18.7 us
  Pallas kernels  18.1 us (96%)
  between operations  0.64 us (3%)
    pallas_call x1, Pallas kernels, per_device(): pl.pallas_call(body, out_shape=tuple((pltpu.VMEM(shape, f32) for shape in...  17.1 us
    pallas_call x1, Pallas kernels, per_device(): pl.pallas_call(write_out, out_shape=tuple((pltpu.HBM(shape, f32) for shap...  0.95 us

profile of v7, /device:TPU:1, one launch (start us, length us, event | category | flops | bytes accessed | tf_op | source)
XLA Modules:
  0.0 18.7 jit_solution(15048510815353249078)
XLA Ops:
  0.6 17.1 %shard_map.112 = (f32[2,24,32,128]{3,2,1,0:T(8,128)S(1)}, f32[8,16,128]{2,1,0:T(8,128)S(1)}, f32[2,8,16,128]{3,2,1,0:T(8,128)S(1)}) custom-call(f32[4,6]{1,0:T(4,128)} %bitcast.4, f32[2,8]{1,0:T(2,128)} %okappa_in.1, f32[2,6]{1,0:T(2,128)} %gain_in.1, s32[1,16]{1,0:T(1,128)} %bitcast.5, f32[6,4,32,256]{3,2,1,0:T(8,128)} %atm.1, f32[32,256]{1,0:T(8,128)} %iw_in.1, ...), custom_call_target="tpu_custom_call" | custom-call | tf_op jit(solution)/shard_map/pallas_call | solution.py:663
  17.8 1.0 %shard_map.113 = (f32[6,4,32,256]{3,2,1,0:T(8,128)}, f32[6,16,128]{2,1,0:T(8,128)}, f32[2,8,16,128]{3,2,1,0:T(8,128)}) custom-call(f32[2,24,32,128]{3,2,1,0:T(8,128)S(1)} %get-tuple-element.6.outst, f32[8,16,128]{2,1,0:T(8,128)S(1)} %get-tuple-element.7.fout, f32[2,8,16,128]{3,2,1,0:T(8,128)S(1)} %get-tuple-element.8.oout), custom_call_target="tpu_custom_call" | custom-call | tf_op jit(solution)/shard_map/pallas_call | solution.py:711

commit v8 on v7

--- a/solution.py
+++ b/solution.py
@@ -46,7 +46,7 @@
     c0, h0, c1, h1, c2, h2,
     mnat, ko, live,
     xs, msg, got,
-    in_sem, hs_sem, hr_sem, as_sem, ar_sem,
+    row_sem, in_sem, hs_sem, hr_sem, as_sem, ar_sem,
 ):
     gx = lax.axis_index("gx")
     gy = lax.axis_index("gy")
@@ -91,8 +91,10 @@
             greet(a, b)
     for a, b in ((left, gy), (right, gy), (gx, up), (gx, down)):
         greet(a, b)
-    for k in range(2, GX - 1):
-        greet(lax.rem(gx + k, GX), gy)
+    on_z = [gx // 4 * 4 + lax.rem(gx + k, 4) for k in range(1, 4)]
+    on_y = [lax.rem(gx + 4 * k, GX) for k in range(1, 4)]
+    for a in on_z + on_y:
+        greet(a, gy)
 
     for n in (2, 3, 4):
         for c in ins[n]:
@@ -233,7 +235,7 @@
         sl[4 + j] = jnp.where(c_lo, x[0], pltpu.roll(x[1], 4, 1))
         sr[4 + j] = jnp.where(c_lo, pltpu.roll(x[1], 124, 1), x[0])
 
-    pl.semaphore_wait(barrier, 8 + GX - 3)
+    pl.semaphore_wait(barrier, 8 + 3 + 3)
 
     send(gsl.at[pl.ds(1, 1)], grr.at[pl.ds(0, 1)], G0_DIAG, left, down)
     send(gsl.at[pl.ds(0, 1)], grr.at[pl.ds(3, 1)], G0_DIAG + 1, left, up)
@@ -255,6 +257,11 @@
     send(sr, rl.at[pl.ds(7, 24)], SIDE_LEFT, right, gy)
     send(sd, ru, OC_TOP, gx, down)
     send(su, rd, OC_BOT, gx, up)
+
+    for a in on_y:
+        pl.semaphore_signal(
+            row_sem, inc=1, device_id={"gx": a, "gy": gy}, device_id_type=MESH
+        )
 
     top_flag = jnp.where(gy == 0, 0.0, 1.0).astype(jnp.float32)
     bot_flag = jnp.where(gy == GY - 1, 0.0, 1.0).astype(jnp.float32)
@@ -454,6 +461,7 @@
         )
 
     moves = [remap(k) for k in range(1, GX)]
+    pl.semaphore_wait(row_sem, 3)
     for c in moves[:-1]:
         c.start()
 
@@ -688,6 +696,7 @@
             vm((2, 5, 32, 128), f32),
             vm((OROWS, OCOLS), f32),
             vm((16,) + v, f32), vm((16,) + v, f32), vm((16,) + v, f32),
+            pltpu.SemaphoreType.REGULAR,
             pltpu.SemaphoreType.DMA((18,)),
             pltpu.SemaphoreType.DMA,
             pltpu.SemaphoreType.DMA((4,)),

time: 18.9 us -> 18.9 us (level)
  no operation moved by 1% of the time
where the time goes in v8:
time: 18.9 us; the launch traced here: 18.7 us
  Pallas kernels  18.1 us (96%)
  between operations  0.64 us (3%)
    pallas_call x1, Pallas kernels, per_device(): pl.pallas_call(body, out_shape=tuple((pltpu.VMEM(shape, f32) for shape in...  17.1 us
    pallas_call x1, Pallas kernels, per_device(): pl.pallas_call(write_out, out_shape=tuple((pltpu.HBM(shape, f32) for shap...  0.95 us

profile of v8, /device:TPU:1, one launch (start us, length us, event | category | flops | bytes accessed | tf_op | source)
XLA Modules:
  0.0 18.7 jit_solution(14254182952492176687)
XLA Ops:
  0.6 17.1 %shard_map.112 = (f32[2,24,32,128]{3,2,1,0:T(8,128)S(1)}, f32[8,16,128]{2,1,0:T(8,128)S(1)}, f32[2,8,16,128]{3,2,1,0:T(8,128)S(1)}) custom-call(f32[4,6]{1,0:T(4,128)} %bitcast.4, f32[2,8]{1,0:T(2,128)} %okappa_in.1, f32[2,6]{1,0:T(2,128)} %gain_in.1, s32[1,16]{1,0:T(1,128)} %bitcast.5, f32[6,4,32,256]{3,2,1,0:T(8,128)} %atm.1, f32[32,256]{1,0:T(8,128)} %iw_in.1, ...), custom_call_target="tpu_custom_call" | custom-call | tf_op jit(solution)/shard_map/pallas_call | solution.py:671
  17.8 1.0 %shard_map.113 = (f32[6,4,32,256]{3,2,1,0:T(8,128)}, f32[6,16,128]{2,1,0:T(8,128)}, f32[2,8,16,128]{3,2,1,0:T(8,128)}) custom-call(f32[2,24,32,128]{3,2,1,0:T(8,128)S(1)} %get-tuple-element.6.outst, f32[8,16,128]{2,1,0:T(8,128)S(1)} %get-tuple-element.7.fout, f32[2,8,16,128]{3,2,1,0:T(8,128)S(1)} %get-tuple-element.8.oout), custom_call_target="tpu_custom_call" | custom-call | tf_op jit(solution)/shard_map/pallas_call | solution.py:720
